TPU v7x, 32 devices: a whole 2x2x4 slice. The times are simulated.
32 devices in a mesh: layer: 4 (over y, core), expert: 8 (over z, x).
Axes of the slice: x: 2, y: 2, z: 4, core: 2. Of those that a mesh axis runs over, the one named last changes fastest.
Arguments:
- stream_in: bfloat16 [4, 256, 3584], P(None, 'expert'), may hold values from -6 to 6
- gain: float32 [4, 3584], P('layer'), may hold values from 0.5 to 1.5
- w_gate: bfloat16 [4, 3584, 2048], P('layer', None, 'expert'), may hold values from -0.09375 to 0.09375
- w_up: bfloat16 [4, 3584, 2048], P('layer', None, 'expert'), may hold values from -0.09375 to 0.09375
- w_down: bfloat16 [4, 2048, 3584], P('layer', 'expert'), may hold values from -0.125 to 0.125
- routes: int32 [4, 4, 256, 8], P('layer', None, 'expert'), may hold values from 0 to 255, all different within a row; in each aligned block of 32 rows (0 to 31, 32 to 63, ..., all dimensions but the last counted through in order) at most 2 rows name the same one
- gates: float32 [4, 4, 256, 8], P('layer', None, 'expert'), may hold values from 0.2 to 1
Outputs:
- layer_out: bfloat16 [4, 4, 256, 3584], P('layer', None, 'expert')
- hessian: float32 [4, 2048, 2048], P('layer', 'expert')
Inputs may be any that keep to these rules, and one draw needn't show every extreme that they name: `routes`: each token names 8 different experts; in each aligned block of 32 tokens (the rows of one device) no expert is named by more than 2 tokens.
All inputs are finite; a program needn't handle non-finite values.
Results may differ from a plain program's by a relative error of at most 0.014.
Values may be sent and summed in bfloat16 or wider, within the bound.
No kernel may reach another device: no remote copies, remote signals or barrier semaphores. Data moves between devices by JAX's collectives and lax.ppermute only.
A program may use at most 64 MiB of HBM per device.

v0:
```python
import jax
import jax.numpy as jnp
from jax import lax
from jax.sharding import PartitionSpec as P

GROUP = 8
CAP = 2


EPSILON = 1e-06


def partner(value, axis, bit):
    return lax.ppermute(value, axis, [(i, i ^ 1 << bit) for i in range(lax.axis_size(axis))])


def passed_along(value, axis, by):
    devices = lax.axis_size(axis)
    pairs = [(i, i + by) for i in range(devices) if 0 <= i + by < devices]
    return lax.ppermute(value, axis, pairs)


def normalize(rows, gain_row):
    wide = rows.astype(jnp.float32)
    scale = lax.rsqrt(jnp.mean(wide * wide, axis=-1, keepdims=True) + EPSILON)
    return (wide * scale * gain_row).astype(jnp.bfloat16)


def slot_tables(route_rows, gate_rows, flight, capacity):
    expert_ids = lax.broadcasted_iota(jnp.int32, (1, 1, flight), 2)
    matches = route_rows[:, :, None] == expert_ids
    routed = jnp.any(matches, axis=1)
    weight = jnp.sum(jnp.where(matches, gate_rows[:, :, None], 0.0), axis=1)
    place = jnp.cumsum(routed.astype(jnp.int32), axis=0) - 1
    slot_ids = lax.broadcasted_iota(jnp.int32, (1, 1, capacity), 2)
    select = jnp.logical_and(routed[:, :, None], place[:, :, None] == slot_ids)
    return (select.astype(jnp.bfloat16), weight)


def member_bit(bit):
    return lax.axis_index("expert") >> bit & 1


def share_units(hidden):
    joined = hidden
    for bit in range(GROUP.bit_length() - 1):
        other = partner(joined, "expert", bit)
        upper = member_bit(bit) == 1
        joined = jnp.where(
            upper,
            jnp.concatenate([other, joined], axis=1),
            jnp.concatenate([joined, other], axis=1),
        )
    return joined


def layer_step(current, gain_row, gate_weight, up_weight, down_weight, route_rows, gate_rows):
    devices = lax.axis_size("expert")
    flight = devices // GROUP
    width = current.shape[1]
    normed = normalize(current, gain_row)
    select, weight = slot_tables(route_rows, gate_rows, flight, CAP)
    outbound = jnp.einsum("tfc,td->fcd", select, normed, preferred_element_type=jnp.float32).astype(
        jnp.bfloat16
    )
    outbound = jnp.broadcast_to(outbound[:, None], (flight, GROUP, CAP, width)).reshape(
        devices, CAP, width
    )
    arrived = lax.all_to_all(outbound, "expert", split_axis=0, concat_axis=0, tiled=True)
    rows = arrived.reshape(devices * CAP, width)
    gate_act = jnp.dot(rows, gate_weight, preferred_element_type=jnp.float32)
    up_act = jnp.dot(rows, up_weight, preferred_element_type=jnp.float32)
    hidden = (jax.nn.silu(gate_act) * up_act).astype(jnp.bfloat16)
    every_unit = share_units(hidden)
    gram_term = lax.dot_general(
        hidden, every_unit, (((0,), (0,)), ((), ())), preferred_element_type=jnp.float32
    )
    partial_value = jnp.dot(hidden, down_weight, preferred_element_type=jnp.float32).astype(
        jnp.bfloat16
    )
    returned = lax.all_to_all(
        partial_value.reshape(devices, CAP, width),
        "expert",
        split_axis=0,
        concat_axis=0,
        tiled=True,
    )
    returned = returned.reshape(flight, GROUP, CAP, width)
    picked = jnp.einsum("tfc,fgcd->tfd", select, returned, preferred_element_type=jnp.float32)
    update = jnp.sum(weight[:, :, None] * picked, axis=1)
    following = (current.astype(jnp.float32) + update).astype(jnp.bfloat16)
    return (following, gram_term)


def shards(stream_in, gain, w_gate, w_up, w_down, routes, gates):
    fronts = stream_in.shape[0]
    tok_rows = stream_in.shape[1]
    width = stream_in.shape[2]
    units = w_gate.shape[2]
    sections = lax.axis_size("layer")
    section = lax.axis_index("layer")

    def advance(step, carry):
        incoming, produced, gram = carry
        front = step - section
        valid = jnp.logical_and(front >= 0, front < fronts)
        slot = jnp.clip(front, 0, fronts - 1)
        fresh = lax.dynamic_index_in_dim(
            stream_in, jnp.minimum(step, fronts - 1), 0, keepdims=False
        )
        current = jnp.where(section == 0, fresh, incoming)
        route_rows = lax.dynamic_index_in_dim(routes[0], slot, 0, keepdims=False)
        gate_rows = lax.dynamic_index_in_dim(gates[0], slot, 0, keepdims=False)
        following, gram_term = layer_step(
            current, gain[0], w_gate[0], w_up[0], w_down[0], route_rows, gate_rows
        )
        kept = lax.dynamic_index_in_dim(produced, slot, 0, keepdims=False)
        produced = lax.dynamic_update_index_in_dim(
            produced, jnp.where(valid, following, kept), slot, 0
        )
        gram = gram + jnp.where(valid, gram_term, 0.0)
        incoming = passed_along(following, "layer", 1)
        return (incoming, produced, gram)

    start = (
        jnp.zeros((tok_rows, width), jnp.bfloat16),
        jnp.zeros((fronts, tok_rows, width), jnp.bfloat16),
        jnp.zeros((units, GROUP * units), jnp.float32),
    )
    incoming, produced, gram = lax.fori_loop(0, fronts + sections - 1, advance, start)
    return (produced[None], (gram * (1.0 / (fronts * CAP)))[None])


def solution(mesh):
    return jax.shard_map(
        shards,
        mesh=mesh,
        in_specs=(
            P(None, "expert", None),
            P("layer", None),
            P("layer", None, "expert"),
            P("layer", None, "expert"),
            P("layer", "expert", None),
            P("layer", None, "expert", None),
            P("layer", None, "expert", None),
        ),
        out_specs=(P("layer", None, "expert", None), P("layer", "expert", None)),
        check_vma=False,
    )
```

profile of v0, /device:TPU:1, one launch (start us, length us, event | category | flops | bytes accessed | tf_op | source)
XLA Modules:
  0.0 277.1 jit_solution(1825803559422005198)
XLA Ops:
  1.7 273.9 %while.20 = (s32[]{:T(128)}, bf16[32,3584]{1,0:T(8,128)(2,1)S(1)}, bf16[4,32,3584]{2,1,0:T(8,128)(2,1)}, f32[256,2048]{1,0:T(8,128)S(1)}, pred[]{:T(512)}, /*ind...) while((s32[]{:T(128)}, bf16[32,3584]{1,0:T(8,128)(2,1)S(1)}, ...), condition=%wide.region_6.7_spmd.clone, body=%wide.region_0.6_spmd.clone.sunk | while | flops 109553936 | bytes 22527172 | solution.py:130
  5.6 6.4 %all-to-all-start = ((bf16[8,2,3584]{2,1,0:T(2,128)(2,1)}), bf16[8,2,3584]{2,1,0:T(2,128)(2,1)S(1)}, u32[]{:S(2)}, u32[]{:S(2)}) async-start(bf16[8,2,3584]{2,1,0:T(2,128)(2,1)} %reshape.237), calls=%async_computation | async-start | bytes 229376 | tf_op jit(solution)/shard_map/while/body/eval_jaxpr/all_to_all | solution.py:69
  11.9 6.2 %all-to-all-done = bf16[8,2,3584]{2,1,0:T(2,128)(2,1)S(1)} async-done(((bf16[8,2,3584]{2,1,0:T(2,128)(2,1)}), bf16[8,2,3584]{2,1,0:T(2,128)(2,1)S(1)}, u32[]{:S(2)}, u32[]{:S(2)}) %all-to-all-start) | async-done | bytes 114720 | tf_op jit(solution)/shard_map/while/body/eval_jaxpr/all_to_all | solution.py:69
  18.2 2.0 fusion.66
  23.1 3.4 %all-to-all-start.1 = ((bf16[8,2,3584]{2,1,0:T(2,128)(2,1)}), bf16[8,2,3584]{2,1,0:T(2,128)(2,1)S(1)}, u32[]{:S(2)}, u32[]{:S(2)}) async-start(bf16[8,2,3584]{2,1,0:T(2,128)(2,1)} %reshape.239), calls=%async_computation.1 | async-start | bytes 229376 | tf_op jit(solution)/shard_map/while/body/eval_jaxpr/all_to_all | solution.py:81
  29.5 2.8 %collective-permute-start.3 = (bf16[16,1024]{1,0:T(8,128)(2,1)S(1)}, bf16[16,1024]{1,0:T(8,128)(2,1)S(1)}, u32[]{:S(2)}, u32[]{:S(2)}) collective-permute-start(bf16[16,1024]{1,0:T(8,128)(2,1)S(1)} %maximum_select_fusion.9), channel_id=1, source_target_pairs={{0,4},{1,5},{2,6},{3,7},{4,0},{5,1},{6,2},{7,3},{8,12},{9,13},{10,... | collective-permute-start | bytes 98312 | tf_op jit(solution)/shard_map/while/body/eval_jaxpr/ppermute | solution.py:14
  33.6 6.8 %collective-permute-start = (bf16[32,3584]{1,0:T(8,128)(2,1)S(1)}, bf16[32,3584]{1,0:T(8,128)(2,1)S(1)}, u32[]{:S(2)}, u32[]{:S(2)}) collective-permute-start(bf16[32,3584]{1,0:T(8,128)(2,1)S(1)} %get-tuple-element.460), channel_id=1, source_target_pairs={{0,8},{8,16},{16,24},{1,9},{9,17},{17,25},{2,10},{10,18},{18,26},{... | collective-permute-start | bytes 688136 | tf_op jit(solution)/shard_map/while/body/eval_jaxpr/ppermute | solution.py:20
  41.1 2.3 collective-permute-done
  47.3 3.4 %all-to-all-start = ((bf16[8,2,3584]{2,1,0:T(2,128)(2,1)}), bf16[8,2,3584]{2,1,0:T(2,128)(2,1)S(1)}, u32[]{:S(2)}, u32[]{:S(2)}) async-start(bf16[8,2,3584]{2,1,0:T(2,128)(2,1)} %reshape.237), calls=%async_computation | async-start | bytes 229376 | tf_op jit(solution)/shard_map/while/body/eval_jaxpr/all_to_all | solution.py:69
  50.6 6.0 %all-to-all-done = bf16[8,2,3584]{2,1,0:T(2,128)(2,1)S(1)} async-done(((bf16[8,2,3584]{2,1,0:T(2,128)(2,1)}), bf16[8,2,3584]{2,1,0:T(2,128)(2,1)S(1)}, u32[]{:S(2)}, u32[]{:S(2)}) %all-to-all-start) | async-done | bytes 114720 | tf_op jit(solution)/shard_map/while/body/eval_jaxpr/all_to_all | solution.py:69
  56.7 2.0 fusion.66
  61.6 3.4 %all-to-all-start.1 = ((bf16[8,2,3584]{2,1,0:T(2,128)(2,1)}), bf16[8,2,3584]{2,1,0:T(2,128)(2,1)S(1)}, u32[]{:S(2)}, u32[]{:S(2)}) async-start(bf16[8,2,3584]{2,1,0:T(2,128)(2,1)} %reshape.239), calls=%async_computation.1 | async-start | bytes 229376 | tf_op jit(solution)/shard_map/while/body/eval_jaxpr/all_to_all | solution.py:81
  68.3 2.9 %collective-permute-start.3 = (bf16[16,1024]{1,0:T(8,128)(2,1)S(1)}, bf16[16,1024]{1,0:T(8,128)(2,1)S(1)}, u32[]{:S(2)}, u32[]{:S(2)}) collective-permute-start(bf16[16,1024]{1,0:T(8,128)(2,1)S(1)} %maximum_select_fusion.9), channel_id=1, source_target_pairs={{0,4},{1,5},{2,6},{3,7},{4,0},{5,1},{6,2},{7,3},{8,12},{9,13},{10,... | collective-permute-start | bytes 98312 | tf_op jit(solution)/shard_map/while/body/eval_jaxpr/ppermute | solution.py:14
  72.5 6.6 %collective-permute-start = (bf16[32,3584]{1,0:T(8,128)(2,1)S(1)}, bf16[32,3584]{1,0:T(8,128)(2,1)S(1)}, u32[]{:S(2)}, u32[]{:S(2)}) collective-permute-start(bf16[32,3584]{1,0:T(8,128)(2,1)S(1)} %get-tuple-element.460), channel_id=1, source_target_pairs={{0,8},{8,16},{16,24},{1,9},{9,17},{17,25},{2,10},{10,18},{18,26},{... | collective-permute-start | bytes 688136 | tf_op jit(solution)/shard_map/while/body/eval_jaxpr/ppermute | solution.py:20
  79.8 2.3 collective-permute-done
  86.0 3.4 %all-to-all-start = ((bf16[8,2,3584]{2,1,0:T(2,128)(2,1)}), bf16[8,2,3584]{2,1,0:T(2,128)(2,1)S(1)}, u32[]{:S(2)}, u32[]{:S(2)}) async-start(bf16[8,2,3584]{2,1,0:T(2,128)(2,1)} %reshape.237), calls=%async_computation | async-start | bytes 229376 | tf_op jit(solution)/shard_map/while/body/eval_jaxpr/all_to_all | solution.py:69
  89.4 6.0 %all-to-all-done = bf16[8,2,3584]{2,1,0:T(2,128)(2,1)S(1)} async-done(((bf16[8,2,3584]{2,1,0:T(2,128)(2,1)}), bf16[8,2,3584]{2,1,0:T(2,128)(2,1)S(1)}, u32[]{:S(2)}, u32[]{:S(2)}) %all-to-all-start) | async-done | bytes 114720 | tf_op jit(solution)/shard_map/while/body/eval_jaxpr/all_to_all | solution.py:69
  95.4 2.0 fusion.66
  100.3 3.4 %all-to-all-start.1 = ((bf16[8,2,3584]{2,1,0:T(2,128)(2,1)}), bf16[8,2,3584]{2,1,0:T(2,128)(2,1)S(1)}, u32[]{:S(2)}, u32[]{:S(2)}) async-start(bf16[8,2,3584]{2,1,0:T(2,128)(2,1)} %reshape.239), calls=%async_computation.1 | async-start | bytes 229376 | tf_op jit(solution)/shard_map/while/body/eval_jaxpr/all_to_all | solution.py:81
  106.7 3.1 %collective-permute-start.3 = (bf16[16,1024]{1,0:T(8,128)(2,1)S(1)}, bf16[16,1024]{1,0:T(8,128)(2,1)S(1)}, u32[]{:S(2)}, u32[]{:S(2)}) collective-permute-start(bf16[16,1024]{1,0:T(8,128)(2,1)S(1)} %maximum_select_fusion.9), channel_id=1, source_target_pairs={{0,4},{1,5},{2,6},{3,7},{4,0},{5,1},{6,2},{7,3},{8,12},{9,13},{10,... | collective-permute-start | bytes 98312 | tf_op jit(solution)/shard_map/while/body/eval_jaxpr/ppermute | solution.py:14
  110.9 6.9 %collective-permute-start = (bf16[32,3584]{1,0:T(8,128)(2,1)S(1)}, bf16[32,3584]{1,0:T(8,128)(2,1)S(1)}, u32[]{:S(2)}, u32[]{:S(2)}) collective-permute-start(bf16[32,3584]{1,0:T(8,128)(2,1)S(1)} %get-tuple-element.460), channel_id=1, source_target_pairs={{0,8},{8,16},{16,24},{1,9},{9,17},{17,25},{2,10},{10,18},{18,26},{... | collective-permute-start | bytes 688136 | tf_op jit(solution)/shard_map/while/body/eval_jaxpr/ppermute | solution.py:20
  118.5 2.3 collective-permute-done
  124.7 3.4 %all-to-all-start = ((bf16[8,2,3584]{2,1,0:T(2,128)(2,1)}), bf16[8,2,3584]{2,1,0:T(2,128)(2,1)S(1)}, u32[]{:S(2)}, u32[]{:S(2)}) async-start(bf16[8,2,3584]{2,1,0:T(2,128)(2,1)} %reshape.237), calls=%async_computation | async-start | bytes 229376 | tf_op jit(solution)/shard_map/while/body/eval_jaxpr/all_to_all | solution.py:69
  128.1 6.0 %all-to-all-done = bf16[8,2,3584]{2,1,0:T(2,128)(2,1)S(1)} async-done(((bf16[8,2,3584]{2,1,0:T(2,128)(2,1)}), bf16[8,2,3584]{2,1,0:T(2,128)(2,1)S(1)}, u32[]{:S(2)}, u32[]{:S(2)}) %all-to-all-start) | async-done | bytes 114720 | tf_op jit(solution)/shard_map/while/body/eval_jaxpr/all_to_all | solution.py:69
  139.0 3.4 %all-to-all-start.1 = ((bf16[8,2,3584]{2,1,0:T(2,128)(2,1)}), bf16[8,2,3584]{2,1,0:T(2,128)(2,1)S(1)}, u32[]{:S(2)}, u32[]{:S(2)}) async-start(bf16[8,2,3584]{2,1,0:T(2,128)(2,1)} %reshape.239), calls=%async_computation.1 | async-start | bytes 229376 | tf_op jit(solution)/shard_map/while/body/eval_jaxpr/all_to_all | solution.py:81
  145.4 3.1 %collective-permute-start.3 = (bf16[16,1024]{1,0:T(8,128)(2,1)S(1)}, bf16[16,1024]{1,0:T(8,128)(2,1)S(1)}, u32[]{:S(2)}, u32[]{:S(2)}) collective-permute-start(bf16[16,1024]{1,0:T(8,128)(2,1)S(1)} %maximum_select_fusion.9), channel_id=1, source_target_pairs={{0,4},{1,5},{2,6},{3,7},{4,0},{5,1},{6,2},{7,3},{8,12},{9,13},{10,... | collective-permute-start | bytes 98312 | tf_op jit(solution)/shard_map/while/body/eval_jaxpr/ppermute | solution.py:14
  149.7 6.9 %collective-permute-start = (bf16[32,3584]{1,0:T(8,128)(2,1)S(1)}, bf16[32,3584]{1,0:T(8,128)(2,1)S(1)}, u32[]{:S(2)}, u32[]{:S(2)}) collective-permute-start(bf16[32,3584]{1,0:T(8,128)(2,1)S(1)} %get-tuple-element.460), channel_id=1, source_target_pairs={{0,8},{8,16},{16,24},{1,9},{9,17},{17,25},{2,10},{10,18},{18,26},{... | collective-permute-start | bytes 688136 | tf_op jit(solution)/shard_map/while/body/eval_jaxpr/ppermute | solution.py:20
  157.2 2.3 collective-permute-done
  163.4 3.4 %all-to-all-start = ((bf16[8,2,3584]{2,1,0:T(2,128)(2,1)}), bf16[8,2,3584]{2,1,0:T(2,128)(2,1)S(1)}, u32[]{:S(2)}, u32[]{:S(2)}) async-start(bf16[8,2,3584]{2,1,0:T(2,128)(2,1)} %reshape.237), calls=%async_computation | async-start | bytes 229376 | tf_op jit(solution)/shard_map/while/body/eval_jaxpr/all_to_all | solution.py:69
  166.8 6.0 %all-to-all-done = bf16[8,2,3584]{2,1,0:T(2,128)(2,1)S(1)} async-done(((bf16[8,2,3584]{2,1,0:T(2,128)(2,1)}), bf16[8,2,3584]{2,1,0:T(2,128)(2,1)S(1)}, u32[]{:S(2)}, u32[]{:S(2)}) %all-to-all-start) | async-done | bytes 114720 | tf_op jit(solution)/shard_map/while/body/eval_jaxpr/all_to_all | solution.py:69
  177.7 3.4 %all-to-all-start.1 = ((bf16[8,2,3584]{2,1,0:T(2,128)(2,1)}), bf16[8,2,3584]{2,1,0:T(2,128)(2,1)S(1)}, u32[]{:S(2)}, u32[]{:S(2)}) async-start(bf16[8,2,3584]{2,1,0:T(2,128)(2,1)} %reshape.239), calls=%async_computation.1 | async-start | bytes 229376 | tf_op jit(solution)/shard_map/while/body/eval_jaxpr/all_to_all | solution.py:81
  184.1 3.2 %collective-permute-start.3 = (bf16[16,1024]{1,0:T(8,128)(2,1)S(1)}, bf16[16,1024]{1,0:T(8,128)(2,1)S(1)}, u32[]{:S(2)}, u32[]{:S(2)}) collective-permute-start(bf16[16,1024]{1,0:T(8,128)(2,1)S(1)} %maximum_select_fusion.9), channel_id=1, source_target_pairs={{0,4},{1,5},{2,6},{3,7},{4,0},{5,1},{6,2},{7,3},{8,12},{9,13},{10,... | collective-permute-start | bytes 98312 | tf_op jit(solution)/shard_map/while/body/eval_jaxpr/ppermute | solution.py:14
  188.4 6.8 %collective-permute-start = (bf16[32,3584]{1,0:T(8,128)(2,1)S(1)}, bf16[32,3584]{1,0:T(8,128)(2,1)S(1)}, u32[]{:S(2)}, u32[]{:S(2)}) collective-permute-start(bf16[32,3584]{1,0:T(8,128)(2,1)S(1)} %get-tuple-element.460), channel_id=1, source_target_pairs={{0,8},{8,16},{16,24},{1,9},{9,17},{17,25},{2,10},{10,18},{18,26},{... | collective-permute-start | bytes 688136 | tf_op jit(solution)/shard_map/while/body/eval_jaxpr/ppermute | solution.py:20
  195.9 2.3 collective-permute-done
  202.1 3.4 %all-to-all-start = ((bf16[8,2,3584]{2,1,0:T(2,128)(2,1)}), bf16[8,2,3584]{2,1,0:T(2,128)(2,1)S(1)}, u32[]{:S(2)}, u32[]{:S(2)}) async-start(bf16[8,2,3584]{2,1,0:T(2,128)(2,1)} %reshape.237), calls=%async_computation | async-start | bytes 229376 | tf_op jit(solution)/shard_map/while/body/eval_jaxpr/all_to_all | solution.py:69
  205.5 6.0 %all-to-all-done = bf16[8,2,3584]{2,1,0:T(2,128)(2,1)S(1)} async-done(((bf16[8,2,3584]{2,1,0:T(2,128)(2,1)}), bf16[8,2,3584]{2,1,0:T(2,128)(2,1)S(1)}, u32[]{:S(2)}, u32[]{:S(2)}) %all-to-all-start) | async-done | bytes 114720 | tf_op jit(solution)/shard_map/while/body/eval_jaxpr/all_to_all | solution.py:69
  211.5 2.0 fusion.66
  216.4 3.4 %all-to-all-start.1 = ((bf16[8,2,3584]{2,1,0:T(2,128)(2,1)}), bf16[8,2,3584]{2,1,0:T(2,128)(2,1)S(1)}, u32[]{:S(2)}, u32[]{:S(2)}) async-start(bf16[8,2,3584]{2,1,0:T(2,128)(2,1)} %reshape.239), calls=%async_computation.1 | async-start | bytes 229376 | tf_op jit(solution)/shard_map/while/body/eval_jaxpr/all_to_all | solution.py:81
  222.8 3.3 %collective-permute-start.3 = (bf16[16,1024]{1,0:T(8,128)(2,1)S(1)}, bf16[16,1024]{1,0:T(8,128)(2,1)S(1)}, u32[]{:S(2)}, u32[]{:S(2)}) collective-permute-start(bf16[16,1024]{1,0:T(8,128)(2,1)S(1)} %maximum_select_fusion.9), channel_id=1, source_target_pairs={{0,4},{1,5},{2,6},{3,7},{4,0},{5,1},{6,2},{7,3},{8,12},{9,13},{10,... | collective-permute-start | bytes 98312 | tf_op jit(solution)/shard_map/while/body/eval_jaxpr/ppermute | solution.py:14
  227.2 6.7 %collective-permute-start = (bf16[32,3584]{1,0:T(8,128)(2,1)S(1)}, bf16[32,3584]{1,0:T(8,128)(2,1)S(1)}, u32[]{:S(2)}, u32[]{:S(2)}) collective-permute-start(bf16[32,3584]{1,0:T(8,128)(2,1)S(1)} %get-tuple-element.460), channel_id=1, source_target_pairs={{0,8},{8,16},{16,24},{1,9},{9,17},{17,25},{2,10},{10,18},{18,26},{... | collective-permute-start | bytes 688136 | tf_op jit(solution)/shard_map/while/body/eval_jaxpr/ppermute | solution.py:20
  234.6 2.3 collective-permute-done
  240.8 3.4 %all-to-all-start = ((bf16[8,2,3584]{2,1,0:T(2,128)(2,1)}), bf16[8,2,3584]{2,1,0:T(2,128)(2,1)S(1)}, u32[]{:S(2)}, u32[]{:S(2)}) async-start(bf16[8,2,3584]{2,1,0:T(2,128)(2,1)} %reshape.237), calls=%async_computation | async-start | bytes 229376 | tf_op jit(solution)/shard_map/while/body/eval_jaxpr/all_to_all | solution.py:69
  244.2 6.0 %all-to-all-done = bf16[8,2,3584]{2,1,0:T(2,128)(2,1)S(1)} async-done(((bf16[8,2,3584]{2,1,0:T(2,128)(2,1)}), bf16[8,2,3584]{2,1,0:T(2,128)(2,1)S(1)}, u32[]{:S(2)}, u32[]{:S(2)}) %all-to-all-start) | async-done | bytes 114720 | tf_op jit(solution)/shard_map/while/body/eval_jaxpr/all_to_all | solution.py:69
  250.2 2.0 fusion.66
  255.1 3.4 %all-to-all-start.1 = ((bf16[8,2,3584]{2,1,0:T(2,128)(2,1)}), bf16[8,2,3584]{2,1,0:T(2,128)(2,1)S(1)}, u32[]{:S(2)}, u32[]{:S(2)}) async-start(bf16[8,2,3584]{2,1,0:T(2,128)(2,1)} %reshape.239), calls=%async_computation.1 | async-start | bytes 229376 | tf_op jit(solution)/shard_map/while/body/eval_jaxpr/all_to_all | solution.py:81
  261.5 3.4 %collective-permute-start.3 = (bf16[16,1024]{1,0:T(8,128)(2,1)S(1)}, bf16[16,1024]{1,0:T(8,128)(2,1)S(1)}, u32[]{:S(2)}, u32[]{:S(2)}) collective-permute-start(bf16[16,1024]{1,0:T(8,128)(2,1)S(1)} %maximum_select_fusion.9), channel_id=1, source_target_pairs={{0,4},{1,5},{2,6},{3,7},{4,0},{5,1},{6,2},{7,3},{8,12},{9,13},{10,... | collective-permute-start | bytes 98312 | tf_op jit(solution)/shard_map/while/body/eval_jaxpr/ppermute | solution.py:14
  266.0 6.6 %collective-permute-start = (bf16[32,3584]{1,0:T(8,128)(2,1)S(1)}, bf16[32,3584]{1,0:T(8,128)(2,1)S(1)}, u32[]{:S(2)}, u32[]{:S(2)}) collective-permute-start(bf16[32,3584]{1,0:T(8,128)(2,1)S(1)} %get-tuple-element.460), channel_id=1, source_target_pairs={{0,8},{8,16},{16,24},{1,9},{9,17},{17,25},{2,10},{10,18},{18,26},{... | collective-permute-start | bytes 688136 | tf_op jit(solution)/shard_map/while/body/eval_jaxpr/ppermute | solution.py:20
  273.3 2.3 collective-permute-done
  (209 shorter events, 88.3 us)
Async XLA Ops:
  5.6 12.5 %all-to-all-start = ((bf16[8,2,3584]{2,1,0:T(2,128)(2,1)}), bf16[8,2,3584]{2,1,0:T(2,128)(2,1)S(1)}, u32[]{:S(2)}, u32[]{:S(2)}) async-start(bf16[8,2,3584]{2,1,0:T(2,128)(2,1)} %reshape.237), calls=%async_computation | async-start | bytes 229376 | tf_op jit(solution)/shard_map/while/body/eval_jaxpr/all_to_all | solution.py:69
  18.2 3.9 %copy-start = (bf16[1,256,3584]{2,1,0:T(8,128)(2,1)S(1)}, bf16[1,256,3584]{2,1,0:T(8,128)(2,1)}, u32[]{:S(2)}) copy-start(bf16[1,256,3584]{2,1,0:T(8,128)(2,1)} %get-tuple-element.516) | copy-start | bytes 5505028 | tf_op jit(solution)/shard_map/while
  22.0 4.4 %collective-permute-start.1 = (bf16[16,256]{1,0:T(8,128)(2,1)S(1)}, bf16[16,256]{1,0:T(8,128)(2,1)S(1)}, u32[]{:S(2)}, u32[]{:S(2)}) collective-permute-start(bf16[16,256]{1,0:T(8,128)(2,1)S(1)} %fusion.67), channel_id=1, source_target_pairs={{0,1},{1,0},{2,3},{3,2},{4,5},{5,4},{6,7},{7,6},{8,9},{9,8},{10,11... | collective-permute-start | bytes 24584 | tf_op jit(solution)/shard_map/while/body/eval_jaxpr/ppermute | solution.py:14
  23.1 9.4 %all-to-all-start.1 = ((bf16[8,2,3584]{2,1,0:T(2,128)(2,1)}), bf16[8,2,3584]{2,1,0:T(2,128)(2,1)S(1)}, u32[]{:S(2)}, u32[]{:S(2)}) async-start(bf16[8,2,3584]{2,1,0:T(2,128)(2,1)} %reshape.239), calls=%async_computation.1 | async-start | bytes 229376 | tf_op jit(solution)/shard_map/while/body/eval_jaxpr/all_to_all | solution.py:81
  26.5 3.0 %collective-permute-start.2 = (bf16[16,512]{1,0:T(8,128)(2,1)S(1)}, bf16[16,512]{1,0:T(8,128)(2,1)S(1)}, u32[]{:S(2)}, u32[]{:S(2)}) collective-permute-start(bf16[16,512]{1,0:T(8,128)(2,1)S(1)} %maximum_select_fusion.8), channel_id=1, source_target_pairs={{0,2},{1,3},{2,0},{3,1},{4,6},{5,7},{6,4},{7,5},{8,10},{9,11},{10,... | collective-permute-start | bytes 49160 | tf_op jit(solution)/shard_map/while/body/eval_jaxpr/ppermute | solution.py:14
  29.5 10.9 %collective-permute-start.3 = (bf16[16,1024]{1,0:T(8,128)(2,1)S(1)}, bf16[16,1024]{1,0:T(8,128)(2,1)S(1)}, u32[]{:S(2)}, u32[]{:S(2)}) collective-permute-start(bf16[16,1024]{1,0:T(8,128)(2,1)S(1)} %maximum_select_fusion.9), channel_id=1, source_target_pairs={{0,4},{1,5},{2,6},{3,7},{4,0},{5,1},{6,2},{7,3},{8,12},{9,13},{10,... | collective-permute-start | bytes 98312 | tf_op jit(solution)/shard_map/while/body/eval_jaxpr/ppermute | solution.py:14
  33.6 9.8 %collective-permute-start = (bf16[32,3584]{1,0:T(8,128)(2,1)S(1)}, bf16[32,3584]{1,0:T(8,128)(2,1)S(1)}, u32[]{:S(2)}, u32[]{:S(2)}) collective-permute-start(bf16[32,3584]{1,0:T(8,128)(2,1)S(1)} %get-tuple-element.460), channel_id=1, source_target_pairs={{0,8},{8,16},{16,24},{1,9},{9,17},{17,25},{2,10},{10,18},{18,26},{... | collective-permute-start | bytes 688136 | tf_op jit(solution)/shard_map/while/body/eval_jaxpr/ppermute | solution.py:20
  47.3 9.4 %all-to-all-start = ((bf16[8,2,3584]{2,1,0:T(2,128)(2,1)}), bf16[8,2,3584]{2,1,0:T(2,128)(2,1)S(1)}, u32[]{:S(2)}, u32[]{:S(2)}) async-start(bf16[8,2,3584]{2,1,0:T(2,128)(2,1)} %reshape.237), calls=%async_computation | async-start | bytes 229376 | tf_op jit(solution)/shard_map/while/body/eval_jaxpr/all_to_all | solution.py:69
  56.7 3.9 %copy-start = (bf16[1,256,3584]{2,1,0:T(8,128)(2,1)S(1)}, bf16[1,256,3584]{2,1,0:T(8,128)(2,1)}, u32[]{:S(2)}) copy-start(bf16[1,256,3584]{2,1,0:T(8,128)(2,1)} %get-tuple-element.516) | copy-start | bytes 5505028 | tf_op jit(solution)/shard_map/while
  60.6 4.4 %collective-permute-start.1 = (bf16[16,256]{1,0:T(8,128)(2,1)S(1)}, bf16[16,256]{1,0:T(8,128)(2,1)S(1)}, u32[]{:S(2)}, u32[]{:S(2)}) collective-permute-start(bf16[16,256]{1,0:T(8,128)(2,1)S(1)} %fusion.67), channel_id=1, source_target_pairs={{0,1},{1,0},{2,3},{3,2},{4,5},{5,4},{6,7},{7,6},{8,9},{9,8},{10,11... | collective-permute-start | bytes 24584 | tf_op jit(solution)/shard_map/while/body/eval_jaxpr/ppermute | solution.py:14
  61.6 9.8 %all-to-all-start.1 = ((bf16[8,2,3584]{2,1,0:T(2,128)(2,1)}), bf16[8,2,3584]{2,1,0:T(2,128)(2,1)S(1)}, u32[]{:S(2)}, u32[]{:S(2)}) async-start(bf16[8,2,3584]{2,1,0:T(2,128)(2,1)} %reshape.239), calls=%async_computation.1 | async-start | bytes 229376 | tf_op jit(solution)/shard_map/while/body/eval_jaxpr/all_to_all | solution.py:81
  65.0 3.3 %collective-permute-start.2 = (bf16[16,512]{1,0:T(8,128)(2,1)S(1)}, bf16[16,512]{1,0:T(8,128)(2,1)S(1)}, u32[]{:S(2)}, u32[]{:S(2)}) collective-permute-start(bf16[16,512]{1,0:T(8,128)(2,1)S(1)} %maximum_select_fusion.8), channel_id=1, source_target_pairs={{0,2},{1,3},{2,0},{3,1},{4,6},{5,7},{6,4},{7,5},{8,10},{9,11},{10,... | collective-permute-start | bytes 49160 | tf_op jit(solution)/shard_map/while/body/eval_jaxpr/ppermute | solution.py:14
  68.3 10.8 %collective-permute-start.3 = (bf16[16,1024]{1,0:T(8,128)(2,1)S(1)}, bf16[16,1024]{1,0:T(8,128)(2,1)S(1)}, u32[]{:S(2)}, u32[]{:S(2)}) collective-permute-start(bf16[16,1024]{1,0:T(8,128)(2,1)S(1)} %maximum_select_fusion.9), channel_id=1, source_target_pairs={{0,4},{1,5},{2,6},{3,7},{4,0},{5,1},{6,2},{7,3},{8,12},{9,13},{10,... | collective-permute-start | bytes 98312 | tf_op jit(solution)/shard_map/while/body/eval_jaxpr/ppermute | solution.py:14
  72.5 9.6 %collective-permute-start = (bf16[32,3584]{1,0:T(8,128)(2,1)S(1)}, bf16[32,3584]{1,0:T(8,128)(2,1)S(1)}, u32[]{:S(2)}, u32[]{:S(2)}) collective-permute-start(bf16[32,3584]{1,0:T(8,128)(2,1)S(1)} %get-tuple-element.460), channel_id=1, source_target_pairs={{0,8},{8,16},{16,24},{1,9},{9,17},{17,25},{2,10},{10,18},{18,26},{... | collective-permute-start | bytes 688136 | tf_op jit(solution)/shard_map/while/body/eval_jaxpr/ppermute | solution.py:20
  86.0 9.4 %all-to-all-start = ((bf16[8,2,3584]{2,1,0:T(2,128)(2,1)}), bf16[8,2,3584]{2,1,0:T(2,128)(2,1)S(1)}, u32[]{:S(2)}, u32[]{:S(2)}) async-start(bf16[8,2,3584]{2,1,0:T(2,128)(2,1)} %reshape.237), calls=%async_computation | async-start | bytes 229376 | tf_op jit(solution)/shard_map/while/body/eval_jaxpr/all_to_all | solution.py:69
  95.4 3.9 %copy-start = (bf16[1,256,3584]{2,1,0:T(8,128)(2,1)S(1)}, bf16[1,256,3584]{2,1,0:T(8,128)(2,1)}, u32[]{:S(2)}) copy-start(bf16[1,256,3584]{2,1,0:T(8,128)(2,1)} %get-tuple-element.516) | copy-start | bytes 5505028 | tf_op jit(solution)/shard_map/while
  99.3 4.4 %collective-permute-start.1 = (bf16[16,256]{1,0:T(8,128)(2,1)S(1)}, bf16[16,256]{1,0:T(8,128)(2,1)S(1)}, u32[]{:S(2)}, u32[]{:S(2)}) collective-permute-start(bf16[16,256]{1,0:T(8,128)(2,1)S(1)} %fusion.67), channel_id=1, source_target_pairs={{0,1},{1,0},{2,3},{3,2},{4,5},{5,4},{6,7},{7,6},{8,9},{9,8},{10,11... | collective-permute-start | bytes 24584 | tf_op jit(solution)/shard_map/while/body/eval_jaxpr/ppermute | solution.py:14
  100.3 9.5 %all-to-all-start.1 = ((bf16[8,2,3584]{2,1,0:T(2,128)(2,1)}), bf16[8,2,3584]{2,1,0:T(2,128)(2,1)S(1)}, u32[]{:S(2)}, u32[]{:S(2)}) async-start(bf16[8,2,3584]{2,1,0:T(2,128)(2,1)} %reshape.239), calls=%async_computation.1 | async-start | bytes 229376 | tf_op jit(solution)/shard_map/while/body/eval_jaxpr/all_to_all | solution.py:81
  103.7 3.0 %collective-permute-start.2 = (bf16[16,512]{1,0:T(8,128)(2,1)S(1)}, bf16[16,512]{1,0:T(8,128)(2,1)S(1)}, u32[]{:S(2)}, u32[]{:S(2)}) collective-permute-start(bf16[16,512]{1,0:T(8,128)(2,1)S(1)} %maximum_select_fusion.8), channel_id=1, source_target_pairs={{0,2},{1,3},{2,0},{3,1},{4,6},{5,7},{6,4},{7,5},{8,10},{9,11},{10,... | collective-permute-start | bytes 49160 | tf_op jit(solution)/shard_map/while/body/eval_jaxpr/ppermute | solution.py:14
  106.7 11.1 %collective-permute-start.3 = (bf16[16,1024]{1,0:T(8,128)(2,1)S(1)}, bf16[16,1024]{1,0:T(8,128)(2,1)S(1)}, u32[]{:S(2)}, u32[]{:S(2)}) collective-permute-start(bf16[16,1024]{1,0:T(8,128)(2,1)S(1)} %maximum_select_fusion.9), channel_id=1, source_target_pairs={{0,4},{1,5},{2,6},{3,7},{4,0},{5,1},{6,2},{7,3},{8,12},{9,13},{10,... | collective-permute-start | bytes 98312 | tf_op jit(solution)/shard_map/while/body/eval_jaxpr/ppermute | solution.py:14
  110.9 9.9 %collective-permute-start = (bf16[32,3584]{1,0:T(8,128)(2,1)S(1)}, bf16[32,3584]{1,0:T(8,128)(2,1)S(1)}, u32[]{:S(2)}, u32[]{:S(2)}) collective-permute-start(bf16[32,3584]{1,0:T(8,128)(2,1)S(1)} %get-tuple-element.460), channel_id=1, source_target_pairs={{0,8},{8,16},{16,24},{1,9},{9,17},{17,25},{2,10},{10,18},{18,26},{... | collective-permute-start | bytes 688136 | tf_op jit(solution)/shard_map/while/body/eval_jaxpr/ppermute | solution.py:20
  124.7 9.4 %all-to-all-start = ((bf16[8,2,3584]{2,1,0:T(2,128)(2,1)}), bf16[8,2,3584]{2,1,0:T(2,128)(2,1)S(1)}, u32[]{:S(2)}, u32[]{:S(2)}) async-start(bf16[8,2,3584]{2,1,0:T(2,128)(2,1)} %reshape.237), calls=%async_computation | async-start | bytes 229376 | tf_op jit(solution)/shard_map/while/body/eval_jaxpr/all_to_all | solution.py:69
  134.1 3.9 %copy-start = (bf16[1,256,3584]{2,1,0:T(8,128)(2,1)S(1)}, bf16[1,256,3584]{2,1,0:T(8,128)(2,1)}, u32[]{:S(2)}) copy-start(bf16[1,256,3584]{2,1,0:T(8,128)(2,1)} %get-tuple-element.516) | copy-start | bytes 5505028 | tf_op jit(solution)/shard_map/while
  138.0 4.4 %collective-permute-start.1 = (bf16[16,256]{1,0:T(8,128)(2,1)S(1)}, bf16[16,256]{1,0:T(8,128)(2,1)S(1)}, u32[]{:S(2)}, u32[]{:S(2)}) collective-permute-start(bf16[16,256]{1,0:T(8,128)(2,1)S(1)} %fusion.67), channel_id=1, source_target_pairs={{0,1},{1,0},{2,3},{3,2},{4,5},{5,4},{6,7},{7,6},{8,9},{9,8},{10,11... | collective-permute-start | bytes 24584 | tf_op jit(solution)/shard_map/while/body/eval_jaxpr/ppermute | solution.py:14
  139.0 9.5 %all-to-all-start.1 = ((bf16[8,2,3584]{2,1,0:T(2,128)(2,1)}), bf16[8,2,3584]{2,1,0:T(2,128)(2,1)S(1)}, u32[]{:S(2)}, u32[]{:S(2)}) async-start(bf16[8,2,3584]{2,1,0:T(2,128)(2,1)} %reshape.239), calls=%async_computation.1 | async-start | bytes 229376 | tf_op jit(solution)/shard_map/while/body/eval_jaxpr/all_to_all | solution.py:81
  142.4 3.0 %collective-permute-start.2 = (bf16[16,512]{1,0:T(8,128)(2,1)S(1)}, bf16[16,512]{1,0:T(8,128)(2,1)S(1)}, u32[]{:S(2)}, u32[]{:S(2)}) collective-permute-start(bf16[16,512]{1,0:T(8,128)(2,1)S(1)} %maximum_select_fusion.8), channel_id=1, source_target_pairs={{0,2},{1,3},{2,0},{3,1},{4,6},{5,7},{6,4},{7,5},{8,10},{9,11},{10,... | collective-permute-start | bytes 49160 | tf_op jit(solution)/shard_map/while/body/eval_jaxpr/ppermute | solution.py:14
  145.4 11.1 %collective-permute-start.3 = (bf16[16,1024]{1,0:T(8,128)(2,1)S(1)}, bf16[16,1024]{1,0:T(8,128)(2,1)S(1)}, u32[]{:S(2)}, u32[]{:S(2)}) collective-permute-start(bf16[16,1024]{1,0:T(8,128)(2,1)S(1)} %maximum_select_fusion.9), channel_id=1, source_target_pairs={{0,4},{1,5},{2,6},{3,7},{4,0},{5,1},{6,2},{7,3},{8,12},{9,13},{10,... | collective-permute-start | bytes 98312 | tf_op jit(solution)/shard_map/while/body/eval_jaxpr/ppermute | solution.py:14
  149.7 9.8 %collective-permute-start = (bf16[32,3584]{1,0:T(8,128)(2,1)S(1)}, bf16[32,3584]{1,0:T(8,128)(2,1)S(1)}, u32[]{:S(2)}, u32[]{:S(2)}) collective-permute-start(bf16[32,3584]{1,0:T(8,128)(2,1)S(1)} %get-tuple-element.460), channel_id=1, source_target_pairs={{0,8},{8,16},{16,24},{1,9},{9,17},{17,25},{2,10},{10,18},{18,26},{... | collective-permute-start | bytes 688136 | tf_op jit(solution)/shard_map/while/body/eval_jaxpr/ppermute | solution.py:20
  163.4 9.4 %all-to-all-start = ((bf16[8,2,3584]{2,1,0:T(2,128)(2,1)}), bf16[8,2,3584]{2,1,0:T(2,128)(2,1)S(1)}, u32[]{:S(2)}, u32[]{:S(2)}) async-start(bf16[8,2,3584]{2,1,0:T(2,128)(2,1)} %reshape.237), calls=%async_computation | async-start | bytes 229376 | tf_op jit(solution)/shard_map/while/body/eval_jaxpr/all_to_all | solution.py:69
  172.8 3.9 %copy-start = (bf16[1,256,3584]{2,1,0:T(8,128)(2,1)S(1)}, bf16[1,256,3584]{2,1,0:T(8,128)(2,1)}, u32[]{:S(2)}) copy-start(bf16[1,256,3584]{2,1,0:T(8,128)(2,1)} %get-tuple-element.516) | copy-start | bytes 5505028 | tf_op jit(solution)/shard_map/while
  176.7 4.4 %collective-permute-start.1 = (bf16[16,256]{1,0:T(8,128)(2,1)S(1)}, bf16[16,256]{1,0:T(8,128)(2,1)S(1)}, u32[]{:S(2)}, u32[]{:S(2)}) collective-permute-start(bf16[16,256]{1,0:T(8,128)(2,1)S(1)} %fusion.67), channel_id=1, source_target_pairs={{0,1},{1,0},{2,3},{3,2},{4,5},{5,4},{6,7},{7,6},{8,9},{9,8},{10,11... | collective-permute-start | bytes 24584 | tf_op jit(solution)/shard_map/while/body/eval_jaxpr/ppermute | solution.py:14
  177.7 9.6 %all-to-all-start.1 = ((bf16[8,2,3584]{2,1,0:T(2,128)(2,1)}), bf16[8,2,3584]{2,1,0:T(2,128)(2,1)S(1)}, u32[]{:S(2)}, u32[]{:S(2)}) async-start(bf16[8,2,3584]{2,1,0:T(2,128)(2,1)} %reshape.239), calls=%async_computation.1 | async-start | bytes 229376 | tf_op jit(solution)/shard_map/while/body/eval_jaxpr/all_to_all | solution.py:81
  181.1 3.0 %collective-permute-start.2 = (bf16[16,512]{1,0:T(8,128)(2,1)S(1)}, bf16[16,512]{1,0:T(8,128)(2,1)S(1)}, u32[]{:S(2)}, u32[]{:S(2)}) collective-permute-start(bf16[16,512]{1,0:T(8,128)(2,1)S(1)} %maximum_select_fusion.8), channel_id=1, source_target_pairs={{0,2},{1,3},{2,0},{3,1},{4,6},{5,7},{6,4},{7,5},{8,10},{9,11},{10,... | collective-permute-start | bytes 49160 | tf_op jit(solution)/shard_map/while/body/eval_jaxpr/ppermute | solution.py:14
  184.1 11.1 %collective-permute-start.3 = (bf16[16,1024]{1,0:T(8,128)(2,1)S(1)}, bf16[16,1024]{1,0:T(8,128)(2,1)S(1)}, u32[]{:S(2)}, u32[]{:S(2)}) collective-permute-start(bf16[16,1024]{1,0:T(8,128)(2,1)S(1)} %maximum_select_fusion.9), channel_id=1, source_target_pairs={{0,4},{1,5},{2,6},{3,7},{4,0},{5,1},{6,2},{7,3},{8,12},{9,13},{10,... | collective-permute-start | bytes 98312 | tf_op jit(solution)/shard_map/while/body/eval_jaxpr/ppermute | solution.py:14
  188.4 9.7 %collective-permute-start = (bf16[32,3584]{1,0:T(8,128)(2,1)S(1)}, bf16[32,3584]{1,0:T(8,128)(2,1)S(1)}, u32[]{:S(2)}, u32[]{:S(2)}) collective-permute-start(bf16[32,3584]{1,0:T(8,128)(2,1)S(1)} %get-tuple-element.460), channel_id=1, source_target_pairs={{0,8},{8,16},{16,24},{1,9},{9,17},{17,25},{2,10},{10,18},{18,26},{... | collective-permute-start | bytes 688136 | tf_op jit(solution)/shard_map/while/body/eval_jaxpr/ppermute | solution.py:20
  202.1 9.4 %all-to-all-start = ((bf16[8,2,3584]{2,1,0:T(2,128)(2,1)}), bf16[8,2,3584]{2,1,0:T(2,128)(2,1)S(1)}, u32[]{:S(2)}, u32[]{:S(2)}) async-start(bf16[8,2,3584]{2,1,0:T(2,128)(2,1)} %reshape.237), calls=%async_computation | async-start | bytes 229376 | tf_op jit(solution)/shard_map/while/body/eval_jaxpr/all_to_all | solution.py:69
  211.5 3.9 %copy-start = (bf16[1,256,3584]{2,1,0:T(8,128)(2,1)S(1)}, bf16[1,256,3584]{2,1,0:T(8,128)(2,1)}, u32[]{:S(2)}) copy-start(bf16[1,256,3584]{2,1,0:T(8,128)(2,1)} %get-tuple-element.516) | copy-start | bytes 5505028 | tf_op jit(solution)/shard_map/while
  215.4 4.4 %collective-permute-start.1 = (bf16[16,256]{1,0:T(8,128)(2,1)S(1)}, bf16[16,256]{1,0:T(8,128)(2,1)S(1)}, u32[]{:S(2)}, u32[]{:S(2)}) collective-permute-start(bf16[16,256]{1,0:T(8,128)(2,1)S(1)} %fusion.67), channel_id=1, source_target_pairs={{0,1},{1,0},{2,3},{3,2},{4,5},{5,4},{6,7},{7,6},{8,9},{9,8},{10,11... | collective-permute-start | bytes 24584 | tf_op jit(solution)/shard_map/while/body/eval_jaxpr/ppermute | solution.py:14
  216.4 9.7 %all-to-all-start.1 = ((bf16[8,2,3584]{2,1,0:T(2,128)(2,1)}), bf16[8,2,3584]{2,1,0:T(2,128)(2,1)S(1)}, u32[]{:S(2)}, u32[]{:S(2)}) async-start(bf16[8,2,3584]{2,1,0:T(2,128)(2,1)} %reshape.239), calls=%async_computation.1 | async-start | bytes 229376 | tf_op jit(solution)/shard_map/while/body/eval_jaxpr/all_to_all | solution.py:81
  219.8 3.0 %collective-permute-start.2 = (bf16[16,512]{1,0:T(8,128)(2,1)S(1)}, bf16[16,512]{1,0:T(8,128)(2,1)S(1)}, u32[]{:S(2)}, u32[]{:S(2)}) collective-permute-start(bf16[16,512]{1,0:T(8,128)(2,1)S(1)} %maximum_select_fusion.8), channel_id=1, source_target_pairs={{0,2},{1,3},{2,0},{3,1},{4,6},{5,7},{6,4},{7,5},{8,10},{9,11},{10,... | collective-permute-start | bytes 49160 | tf_op jit(solution)/shard_map/while/body/eval_jaxpr/ppermute | solution.py:14
  222.8 11.1 %collective-permute-start.3 = (bf16[16,1024]{1,0:T(8,128)(2,1)S(1)}, bf16[16,1024]{1,0:T(8,128)(2,1)S(1)}, u32[]{:S(2)}, u32[]{:S(2)}) collective-permute-start(bf16[16,1024]{1,0:T(8,128)(2,1)S(1)} %maximum_select_fusion.9), channel_id=1, source_target_pairs={{0,4},{1,5},{2,6},{3,7},{4,0},{5,1},{6,2},{7,3},{8,12},{9,13},{10,... | collective-permute-start | bytes 98312 | tf_op jit(solution)/shard_map/while/body/eval_jaxpr/ppermute | solution.py:14
  227.2 9.7 %collective-permute-start = (bf16[32,3584]{1,0:T(8,128)(2,1)S(1)}, bf16[32,3584]{1,0:T(8,128)(2,1)S(1)}, u32[]{:S(2)}, u32[]{:S(2)}) collective-permute-start(bf16[32,3584]{1,0:T(8,128)(2,1)S(1)} %get-tuple-element.460), channel_id=1, source_target_pairs={{0,8},{8,16},{16,24},{1,9},{9,17},{17,25},{2,10},{10,18},{18,26},{... | collective-permute-start | bytes 688136 | tf_op jit(solution)/shard_map/while/body/eval_jaxpr/ppermute | solution.py:20
  240.8 9.4 %all-to-all-start = ((bf16[8,2,3584]{2,1,0:T(2,128)(2,1)}), bf16[8,2,3584]{2,1,0:T(2,128)(2,1)S(1)}, u32[]{:S(2)}, u32[]{:S(2)}) async-start(bf16[8,2,3584]{2,1,0:T(2,128)(2,1)} %reshape.237), calls=%async_computation | async-start | bytes 229376 | tf_op jit(solution)/shard_map/while/body/eval_jaxpr/all_to_all | solution.py:69
  254.1 4.4 %collective-permute-start.1 = (bf16[16,256]{1,0:T(8,128)(2,1)S(1)}, bf16[16,256]{1,0:T(8,128)(2,1)S(1)}, u32[]{:S(2)}, u32[]{:S(2)}) collective-permute-start(bf16[16,256]{1,0:T(8,128)(2,1)S(1)} %fusion.67), channel_id=1, source_target_pairs={{0,1},{1,0},{2,3},{3,2},{4,5},{5,4},{6,7},{7,6},{8,9},{9,8},{10,11... | collective-permute-start | bytes 24584 | tf_op jit(solution)/shard_map/while/body/eval_jaxpr/ppermute | solution.py:14
  255.1 9.8 %all-to-all-start.1 = ((bf16[8,2,3584]{2,1,0:T(2,128)(2,1)}), bf16[8,2,3584]{2,1,0:T(2,128)(2,1)S(1)}, u32[]{:S(2)}, u32[]{:S(2)}) async-start(bf16[8,2,3584]{2,1,0:T(2,128)(2,1)} %reshape.239), calls=%async_computation.1 | async-start | bytes 229376 | tf_op jit(solution)/shard_map/while/body/eval_jaxpr/all_to_all | solution.py:81
  258.6 3.0 %collective-permute-start.2 = (bf16[16,512]{1,0:T(8,128)(2,1)S(1)}, bf16[16,512]{1,0:T(8,128)(2,1)S(1)}, u32[]{:S(2)}, u32[]{:S(2)}) collective-permute-start(bf16[16,512]{1,0:T(8,128)(2,1)S(1)} %maximum_select_fusion.8), channel_id=1, source_target_pairs={{0,2},{1,3},{2,0},{3,1},{4,6},{5,7},{6,4},{7,5},{8,10},{9,11},{10,... | collective-permute-start | bytes 49160 | tf_op jit(solution)/shard_map/while/body/eval_jaxpr/ppermute | solution.py:14
  261.5 11.1 %collective-permute-start.3 = (bf16[16,1024]{1,0:T(8,128)(2,1)S(1)}, bf16[16,1024]{1,0:T(8,128)(2,1)S(1)}, u32[]{:S(2)}, u32[]{:S(2)}) collective-permute-start(bf16[16,1024]{1,0:T(8,128)(2,1)S(1)} %maximum_select_fusion.9), channel_id=1, source_target_pairs={{0,4},{1,5},{2,6},{3,7},{4,0},{5,1},{6,2},{7,3},{8,12},{9,13},{10,... | collective-permute-start | bytes 98312 | tf_op jit(solution)/shard_map/while/body/eval_jaxpr/ppermute | solution.py:14
  266.0 9.6 %collective-permute-start = (bf16[32,3584]{1,0:T(8,128)(2,1)S(1)}, bf16[32,3584]{1,0:T(8,128)(2,1)S(1)}, u32[]{:S(2)}, u32[]{:S(2)}) collective-permute-start(bf16[32,3584]{1,0:T(8,128)(2,1)S(1)} %get-tuple-element.460), channel_id=1, source_target_pairs={{0,8},{8,16},{16,24},{1,9},{9,17},{17,25},{2,10},{10,18},{18,26},{... | collective-permute-start | bytes 688136 | tf_op jit(solution)/shard_map/while/body/eval_jaxpr/ppermute | solution.py:20
  (1 other events, 3.9 us)
where the time goes:
time: 280 us; the launch traced here: 277 us
  starting transfers between devices  129 us (46%)
  waiting for transfers between devices  63 us (22%)
  matrix products  42.7 us (15%)
  other arithmetic  22.1 us (8%)
  local copies, waits for them, and re-layouts  18.6 us (7%)
    ppermute x7, starting transfers between devices, passed_along(): return lax.ppermute(value, axis, pairs)  47.4 us
    all_to_all x7, waiting for transfers between devices, layer_step(): lax.all_to_all(outbound, 'expert', split_axis=0, concat_axis=0, tiled=True)  42.3 us
    ppermute x21, starting transfers between devices, partner(): lax.ppermute(value, axis, [(i, i ^ 1 << bit) for i in range(lax.axis_size...  31.7 us
    all_to_all x7, starting transfers between devices, layer_step(): lax.all_to_all(outbound, 'expert', split_axis=0, concat_axis=0, tiled=True)  26.6 us
    all_to_all x7, starting transfers between devices, layer_step(): lax.all_to_all(partial_value.reshape(devices, CAP, width), 'expert', spli...  23.6 us
    ppermute x7, waiting for transfers between devices, passed_along(): return lax.ppermute(value, axis, pairs)  15.9 us
    dot_general x7, matrix products, layer_step(): gate_act = jnp.dot(rows, gate_weight, preferred_element_type=jnp.float32)  13.9 us
    dot_general x7, matrix products, layer_step(): up_act = jnp.dot(rows, up_weight, preferred_element_type=jnp.float32)  13 us
  transfers between devices with their start and end apart: 42, of which 23 were waited for; matrix products, arithmetic and copies ran while one was open for 10% of the time, Pallas kernels for 0%

commit v1 on v0

v1 whole, which is shorter than its diff:
```python
import functools

import jax
import jax.numpy as jnp
from jax import lax
from jax.experimental import pallas as pl
from jax.experimental.pallas import tpu as pltpu
from jax.sharding import PartitionSpec as P

GROUP = 8
CAP = 2
EPSILON = 1e-06
LANES = 128
CHUNK = 128

FEW = 4

STATUS, SOURCE_LAYER, SOURCE_SLOT, WANTED, FULL, DEEP, DEVICE, SLOT, MORE, COUNTS = range(64, 74)
READY, WAITS = 1.0, 2.0

f32 = jnp.float32
bf16 = jnp.bfloat16
VMEM = pl.BlockSpec(memory_space=pltpu.VMEM)
SMEM = pl.BlockSpec(memory_space=pltpu.SMEM)
HBM = pl.BlockSpec(memory_space=pltpu.HBM)


def call(
    body, out_shape, n_in, scalars=0, scratch=(), flops=0, traffic=0, limit=2 * 2**20, streamed=0, placed=None
):
    return pl.pallas_call(
        body,
        out_shape=out_shape,
        in_specs=[SMEM] * scalars + [VMEM] * n_in + [HBM] * streamed,
        out_specs=placed or jax.tree.map(lambda s: VMEM, out_shape),
        scratch_shapes=list(scratch),
        compiler_params=pltpu.CompilerParams(vmem_limit_bytes=limit),
        cost_estimate=pl.CostEstimate(flops=flops, bytes_accessed=traffic, transcendentals=0),
    )


def iota(shape, dim):
    return lax.broadcasted_iota(jnp.int32, shape, dim)


def stack_rows(rows):
    return jnp.concatenate(rows, axis=0)


def lane_of(extra, number):
    return extra[:, number:number + 1]


def across(column):
    size = column.shape[0]
    same = iota((size, size), 0) == iota((size, size), 1)
    return jnp.sum(jnp.where(same, column, 0.0), axis=0, keepdims=True)


def ranked(rows):
    size = rows[0].shape[1]
    upto = (iota((size, size), 0) <= iota((size, size), 1)).astype(f32).astype(bf16)
    rank = jnp.dot(stack_rows(rows).astype(bf16), upto, preferred_element_type=f32)
    return [rank[r:r + 1] * row for r, row in enumerate(rows)]


def selection(rank, count):
    wanted = (iota((count, rank.shape[1]), 0) + 1).astype(f32)
    return jnp.where(rank == wanted, 1.0, 0.0)


def normalized(rows, gain):
    scale = lax.rsqrt(jnp.mean(rows * rows, axis=-1, keepdims=True) + EPSILON)
    return (rows * scale * gain).astype(bf16)


def by_front(routes_ref, of_front):
    return jnp.concatenate([of_front(f) for f in range(routes_ref.shape[0])], axis=1)


def table_body(flight, routes_ref, table_ref, kept_ref):
    kept_ref[...] = routes_ref[...]
    table_ref[...] = by_front(
        routes_ref,
        lambda f: jnp.max(jnp.where(routes_ref[f] < flight, 1.0, 0.0), axis=0, keepdims=True),
    ).astype(bf16)


def held_body(after_ref, *refs):
    count = len(refs) // 2
    sems = refs[-1]
    copies = [pltpu.make_async_copy(refs[i], refs[count + i], sems.at[i]) for i in range(count)]
    for copy in copies:
        copy.start()
    for copy in copies:
        copy.wait()


def rows_body(table_ref, state_ref, raw_ref):
    select = selection(ranked([table_ref[...].astype(f32)])[0], raw_ref.shape[0])
    raw_ref[...] = jnp.dot(select.astype(bf16), state_ref[...], preferred_element_type=f32).astype(bf16)


def gates_body(routes_ref, gates_ref, weights_ref):
    weights_ref[...] = stack_rows([
        by_front(
            routes_ref,
            lambda f: jnp.sum(jnp.where(routes_ref[f] == expert, gates_ref[f], 0.0), axis=0, keepdims=True),
        )
        for expert in range(weights_ref.shape[0])
    ])


def before(layer, a, b):
    return jnp.where((layer ^ a) < (layer ^ b), 1.0, 0.0)


def between(layer, a, b, routed):
    total = jnp.zeros_like(routed[0])
    for r, row in enumerate(routed):
        if r not in (a, b):
            total = jnp.maximum(total, row * before(layer, a, r) * before(layer, r, b))
    return total


def number_of(layer, r, sections):
    return sum(jnp.where((layer ^ r) == other, float(other), 0.0) for other in range(sections))


def meta_body(few, index_ref, *refs):
    tables, (gates_ref, raw_ref, payload_ref) = refs[:-3], refs[-3:]
    layer, member = index_ref[0], index_ref[1]
    count, width = raw_ref.shape
    routed = [ref[...].astype(f32) for ref in tables]
    ranks = ranked(routed)
    waits = source_layer = source_slot = wanted = jnp.zeros_like(routed[0])
    for r in range(1, len(routed)):
        source = routed[r] * before(layer, r, 0) * (1.0 - between(layer, r, 0, routed))
        waits = waits + source
        source_layer = source_layer + source * number_of(layer, r, len(routed))
        source_slot = source_slot + source * ranks[r]
        wanted = jnp.maximum(wanted, routed[r] * before(layer, 0, r))
    status = jnp.where(waits > 0.5, WAITS, READY)
    full = sum(jnp.where(rank > few, 1.0, 0.0) for rank in ranks)
    deep = jnp.where(sum(routed) > 2.5, 1.0, 0.0)
    counts = [jnp.zeros_like(deep) for _ in routed]
    for r, row in enumerate(routed):
        later = jnp.zeros_like(row)
        for other, other_row in enumerate(routed):
            if other != r:
                later = jnp.maximum(later, other_row * before(layer, r, other))
        for place in range(len(counts)):
            counts[place] = counts[place] + row * later * jnp.where((layer ^ r) == place, 1.0, 0.0)
    gates = gates_ref[...]
    high = gates.astype(bf16).astype(f32)
    named = {STATUS: status, SOURCE_LAYER: source_layer, SOURCE_SLOT: source_slot, WANTED: wanted}
    summed = {FULL: full, DEEP: deep}
    summed.update({COUNTS + place: row for place, row in enumerate(counts)})
    for expert in range(gates.shape[0]):
        named[expert] = high[expert:expert + 1]
        named[gates.shape[0] + expert] = (gates - high)[expert:expert + 1]
    select = selection(ranks[0], count)
    across_tokens = (((1,), (1,)), ((), ()))

    def lanes(left, rows):
        empty = jnp.zeros_like(deep)
        table = stack_rows([rows.get(lane, empty) for lane in range(LANES)]).astype(bf16)
        return lax.dot_general(left.astype(bf16), table, across_tokens, preferred_element_type=f32)

    lane = iota((count, LANES), 1)
    extra = lanes(select, named) + lanes(jnp.ones_like(select), summed)
    extra = jnp.where(lane == DEVICE, jnp.full((count, LANES), member + 1, jnp.int32).astype(f32), extra)
    extra = jnp.where(lane == SLOT, (iota((count, LANES), 0) + 1).astype(f32), extra)
    payload_ref[:, :width] = raw_ref[...]
    payload_ref[:, width:] = extra.astype(bf16)


def distances(half):
    return [2 * q for q in range(half)] + [2 * q + 1 for q in range(half)]


def stack_body(half, *refs):
    near, pair_ref, rows_ref = refs[:half], refs[half], refs[half + 1]
    blocks = [ref[...] for ref in near] + [pair_ref[q] for q in range(half)]
    count = blocks[0].shape[0]
    if count % 16 == 0:
        for place, block in enumerate(blocks):
            rows_ref[place * count:(place + 1) * count] = block
    else:
        rows_ref[...] = stack_rows([block.astype(f32) for block in blocks]).astype(bf16)


def first_pass_body(half, sections, count, flight, member_ref, *refs):
    gathered, refs = refs[:half + 1], refs[half + 1:]
    gain_ref, gate_ref, up_ref, down_ref, rows_ref, mode_ref, part_ref, chosen_ref, sent_ref = refs
    stack_body(half, *gathered, rows_ref)
    pass_body(count, flight, member_ref, rows_ref, gain_ref, gate_ref, up_ref, down_ref, part_ref, chosen_ref, sent_ref)
    extra = rows_ref[:, gain_ref.shape[1]:].astype(f32)
    most = jnp.max(extra, axis=0, keepdims=True)
    total = jnp.sum(jnp.where(lane_of(extra, SLOT) == 1.0, extra, 0.0), axis=0, keepdims=True)
    total = jnp.max(total[:, COUNTS:COUNTS + sections], axis=1, keepdims=True)
    wanted_count = part_ref.shape[0]
    mode = sum(jnp.where(total > limit, 1, 0) for limit in (wanted_count // 4, wanted_count // 2, wanted_count))
    mode = jnp.where(lane_of(most, DEEP) > 0.5, 3, mode)
    mode_ref[...] = jnp.where(lane_of(most, FULL) > 0.5, 4, mode)


def activated(rows, gate_ref, up_ref):
    gate = jnp.dot(rows, gate_ref[...], preferred_element_type=f32)
    up = jnp.dot(rows, up_ref[...], preferred_element_type=f32)
    return gate / (1.0 + jnp.exp(-gate)) * up


def weight_of(extra, member, flight):
    lane = iota(extra.shape, 1)
    expert = member // GROUP
    mine = jnp.logical_or(lane == expert, lane == flight + expert)
    return jnp.sum(jnp.where(mine, extra, 0.0), axis=1, keepdims=True)


def pass_body(count, flight, member_ref, rows_ref, gain_ref, gate_ref, up_ref, down_ref, part_ref, chosen_ref, sent_ref):
    member = member_ref[0]
    width = gain_ref.shape[1]
    wanted_count = part_ref.shape[0]
    extra = rows_ref[:, width:].astype(f32)
    wanted = lane_of(extra, WANTED)
    eligible = jnp.where(lane_of(extra, STATUS) == READY, wanted, 0.0)
    number = lane_of(extra, DEVICE) * count + lane_of(extra, SLOT)
    upto = number <= across(number)
    rank = jnp.sum(jnp.where(upto, eligible, 0.0), axis=0, keepdims=True) * across(eligible)
    select = selection(rank, wanted_count)
    chosen = jnp.dot(select.astype(bf16), rows_ref[...], preferred_element_type=f32)
    taken = jnp.sum(select, axis=0, keepdims=True)
    more = jnp.max(across(wanted) - taken, axis=1, keepdims=True)
    sent_ref[...] = taken
    lanes = chosen[:, width:]
    lane = iota(lanes.shape, 1)
    chosen_ref[:, :width] = chosen[:, :width].astype(bf16)
    chosen_ref[:, width:] = jnp.where(lane == MORE, more, lanes).astype(bf16)
    weight = weight_of(lanes, member, flight)
    hidden = activated(normalized(chosen[:, :width], gain_ref[...]), gate_ref, up_ref)
    if flight > 1:
        hidden = jnp.where(weight > 0.0, hidden, 0.0)
    share = jnp.dot(hidden.astype(bf16), down_ref[...], preferred_element_type=f32) * weight
    part_ref[...] = share.astype(bf16)


def added_body(a_ref, b_ref, out_ref):
    out_ref[...] = (a_ref[...].astype(f32) + b_ref[...].astype(f32)).astype(bf16)


def changed_body(a_ref, b_ref, chosen_ref, out_ref):
    width = a_ref.shape[1]
    total = chosen_ref[:, :width].astype(f32) + a_ref[...].astype(f32) + b_ref[...].astype(f32)
    out_ref[:, :width] = total.astype(bf16)
    out_ref[:, width:] = chosen_ref[:, width:]


def by_chunks(size, run):
    if size <= CHUNK:
        run(slice(0, size))
        return

    @pl.loop(0, size // CHUNK)
    def _(i):
        run(pl.ds(pl.multiple_of(i * CHUNK, CHUNK), CHUNK))


def apply_body(sections, layer_ref, rows_ref, sent_ref, *refs):
    changed, into_ref, more_ref = refs[:sections], refs[sections], refs[sections + 1]
    layer = layer_ref[0]
    width = rows_ref.shape[1] - LANES
    names = [ref[:, width:].astype(f32) for ref in changed]
    fresh = stack_rows([ref[:, :width].astype(f32) for ref in changed[1:]]).astype(bf16)
    columns = [(across(lane_of(name, DEVICE)), across(lane_of(name, SLOT))) for name in names]
    more = names[0]
    for name in names[1:]:
        more = jnp.maximum(more, name)
    more_ref[...] = jnp.max(lane_of(more, MORE), axis=0, keepdims=True)
    size = rows_ref.shape[0]
    taken = sent_ref[...]

    def run(part):
        extra = rows_ref[part, width:].astype(f32)
        waits = jnp.where(lane_of(extra, STATUS) == WAITS, 1.0, 0.0)
        matches = []
        for r in range(1, sections):
            device, slot = columns[r]
            match = jnp.where(lane_of(extra, DEVICE) == device, waits, 0.0)
            match = match * jnp.where(lane_of(extra, SOURCE_SLOT) == slot, 1.0, 0.0)
            from_it = jnp.where(lane_of(extra, SOURCE_LAYER) == number_of(layer, r, sections), 1.0, 0.0)
            matches.append(match * from_it)
        match = jnp.concatenate(matches, axis=1)
        arrived = jnp.max(match, axis=1, keepdims=True)
        new = jnp.dot(match.astype(bf16), fresh, preferred_element_type=f32)
        old = rows_ref[part, :width].astype(f32)
        into_ref[part, :width] = jnp.where(arrived > 0.5, new, old).astype(bf16)
        lane = iota(extra.shape, 1)
        extra = jnp.where(jnp.logical_and(lane == STATUS, arrived > 0.5), READY, extra)
        if size <= CHUNK:
            own = iota((size, size), 0) == iota((size, size), 1)
            gone = jnp.sum(jnp.where(own, taken, 0.0), axis=1, keepdims=True)
        else:
            first = part.start
            row = iota((CHUNK, size), 0) + first == iota((CHUNK, size), 1)
            gone = jnp.sum(jnp.where(row, taken, 0.0), axis=1, keepdims=True)
        extra = jnp.where(jnp.logical_and(lane == WANTED, gone > 0.5), 0.0, extra)
        into_ref[part, width:] = extra.astype(bf16)

    by_chunks(size, run)


def changed_final_body(half, sections, flight, layer_ref, member_ref, rows_ref, sent_ref, *refs):
    changed, rest, scratch = refs[:sections], refs[sections:-2], refs[-2:]
    into_ref, more_ref = scratch
    apply_body(sections, layer_ref, rows_ref, sent_ref, *changed, into_ref, more_ref)
    final_body(half, flight, member_ref, into_ref, *rest)


def final_body(half, flight, member_ref, rows_ref, gain_ref, gate_ref, up_ref, down_ref, hidden_ref, raw_ref, near_ref, far_ref, ordered_ref):
    member = member_ref[0]
    width = gain_ref.shape[1]
    units = hidden_ref.shape[1]
    size = rows_ref.shape[0]
    side = size // 2
    count = raw_ref.shape[0]
    raw_ref[...] = rows_ref[:, :width].astype(f32)[:count].astype(bf16) if size <= CHUNK else rows_ref[:count, :width]
    hidden_rows = []

    def run(part, of_part=None):
        extra = rows_ref[part, width:].astype(f32)
        weight = weight_of(extra, member, flight)
        hidden = activated(normalized(rows_ref[part, :width].astype(f32), gain_ref[...]), gate_ref, up_ref)
        if flight > 1:
            hidden = jnp.where(weight > 0.0, hidden, 0.0)
        share = jnp.dot(hidden.astype(bf16), down_ref[...], preferred_element_type=f32) * weight
        return hidden, share.astype(bf16)

    if size <= CHUNK:
        hidden, share = run(slice(0, size))
        near_ref[...] = share[:side]
        far_ref[:, :width] = share[side:]
        for place, r in enumerate(distances(half)):
            ordered_ref[member ^ r, :count] = hidden[place * count:(place + 1) * count]
    else:
        blocks = CHUNK // count

        def half_run(first, into_ref, odd):
            @pl.loop(0, side // CHUNK)
            def _(i):
                at = pl.multiple_of(i * CHUNK, CHUNK)
                hidden, share = run(pl.ds(pl.multiple_of(first + at, CHUNK), CHUNK))
                into_ref[pl.ds(at, CHUNK), :width] = share
                for b in range(blocks):
                    ordered_ref[member ^ (2 * (i * blocks + b) + odd)] = hidden[b * count:(b + 1) * count]

        half_run(0, near_ref, 0)
        half_run(side, far_ref, 1)
    hidden_rows = stack_rows([ordered_ref[source, :count] for source in range(2 * half)]).astype(bf16)
    hidden_ref[...] = hidden_rows
    far_ref[:, width:width + units] = hidden_rows[:side]
    far_ref[:, width + units:] = hidden_rows[side:]


def regrouped(rows, count):
    return jnp.concatenate([rows[i:i + count] for i in range(0, rows.shape[0], count)], axis=1)


def spread(block, units):
    return stack_rows([block[:, i:i + units] for i in range(0, block.shape[1], units)])


def paired_body(half, near_ref, far_ref, hidden_ref, *out_refs):
    width = near_ref.shape[1]
    units = hidden_ref.shape[1]
    count = near_ref.shape[0] // half
    total = near_ref[...].astype(f32) + far_ref[:, :width].astype(f32)
    theirs = far_ref[:, width:].astype(f32)
    both = [hidden_ref[...].astype(f32), theirs[:, :units], theirs[:, units:]]
    both = jnp.concatenate([regrouped(rows, count) for rows in both], axis=1).astype(bf16)
    for q, ref in enumerate(out_refs):
        ref[:, :width] = total[q * count:(q + 1) * count].astype(bf16)
        if ref.shape[1] > width:
            ref[:, width:] = both


def combine_body(half, *refs):
    shares, raw_ref, out_ref = refs[:half], refs[half], refs[-1]
    width = raw_ref.shape[1]
    update = shares[0][:, :width].astype(f32)
    for ref in shares[1:]:
        update = update + ref[:, :width].astype(f32)
    out_ref[...] = (raw_ref[...].astype(f32) + update).astype(bf16)


def merge_body(sections, layer_ref, *refs):
    blocks, tables = refs[:sections], refs[sections:2 * sections]
    state_ref, into_ref, held_ref, sems = refs[2 * sections:]
    layer = layer_ref[0]
    width = state_ref.shape[1]
    count = blocks[0].shape[0]
    routed = [ref[...].astype(f32) for ref in tables]
    shown = [row * jnp.where((layer ^ r) <= layer, 1.0, 0.0) for r, row in enumerate(routed)]
    select = []
    for r, rank in enumerate(ranked(routed)):
        later = jnp.zeros_like(rank)
        for other, row in enumerate(shown):
            if other != r:
                later = jnp.maximum(later, row * before(layer, r, other))
        select.append(selection(jnp.where(shown[r] > 0.5, rank * (1.0 - later), 0.0), count))
    select = stack_rows(select).astype(bf16)
    rows = stack_rows([block[...].astype(f32) for block in blocks]).astype(bf16)
    over = (((0,), (0,)), ((), ()))
    ones = jnp.ones((sections * count, LANES), bf16)
    hit = lax.dot_general(select, ones, over, preferred_element_type=f32)[:, :1]
    copies = []
    chunks = sems.shape[0]
    step = width // chunks
    for i in range(chunks):
        part = slice(i * step, (i + 1) * step)
        fresh = lax.dot_general(select, rows[:, part], over, preferred_element_type=f32)
        held_ref[:, part] = jnp.where(hit > 0.5, fresh.astype(bf16), state_ref[:, part])
        copies.append(pltpu.make_async_copy(held_ref.at[:, part], into_ref.at[:, part], sems.at[i]))
        copies[-1].start()
    for copy in copies:
        copy.wait()


def gram_body(scale, width, member_ref, mine_ref, far_ref, *refs):
    others, (out_ref, held_ref, sem) = refs[:-3], refs[-3:]
    member = member_ref[0] % GROUP
    mine = mine_ref[...]
    size, units = mine.shape
    theirs = far_ref[:, width:]
    blocks = [mine, stack_rows([theirs[:, :units].astype(f32), theirs[:, units:].astype(f32)]).astype(bf16)]
    for ref in others:
        both = spread(ref[:, width:].astype(f32), units).astype(bf16)
        blocks += [both[:size], both[size:]]
    for r, block in enumerate(blocks):
        term = scale * lax.dot_general(
            mine, block, (((0,), (0,)), ((), ())), preferred_element_type=f32
        )
        held_ref[:, pl.ds(pl.multiple_of((member ^ r) * units, units), units)] = term
    copy = pltpu.make_async_copy(held_ref, out_ref, sem)
    copy.start()
    copy.wait()


def passed(value, axis, r):
    return lax.ppermute(value, axis, [(i, i ^ r) for i in range(lax.axis_size(axis))])


def exchanged(value, axis):
    return [value] + [passed(value, axis, r) for r in range(1, lax.axis_size(axis))]


def shards(stream_in, gain, w_gate, w_up, w_down, routes, gates):
    fronts, tok_rows, width = stream_in.shape
    units = w_gate.shape[2]
    sections = lax.axis_size("layer")
    devices = lax.axis_size("expert")
    flight = devices // GROUP
    half = devices // 2
    tokens = fronts * tok_rows
    few = FEW * flight
    shape = jax.ShapeDtypeStruct
    layer = lax.axis_index("layer").astype(jnp.int32).reshape(1)
    member = lax.axis_index("expert").astype(jnp.int32).reshape(1)
    index = jnp.concatenate([layer, member])
    state = stream_in.reshape(tokens, width)
    routes = jnp.swapaxes(routes[0], 1, 2)
    gates = jnp.swapaxes(gates[0], 1, 2)
    w_gate, w_up, w_down = w_gate[0], w_up[0], w_down[0]
    scale = 1.0 / (fronts * CAP)
    mib = 2**20
    chunks = next(c for c in (7, 8, 4, 2, 1) if width % (c * LANES) == 0)

    def payload_of(count, raw, gate_weights):
        return call(
            functools.partial(meta_body, few),
            shape((count, width + LANES), bf16),
            sections + 2,
            scalars=1,
            limit=8 * mib,
        )(index, *tables, gate_weights, raw)

    def pass_shapes(size, wanted):
        return (
            shape((wanted, width), bf16),
            shape((wanted, width + LANES), bf16),
            shape((1, size), f32),
        )

    def pass_limit(size):
        return 8 * mib + 12 * size * width + 32 * size * size

    def summed(part, chosen):
        bits = [1 << b for b in range(devices.bit_length() - 1)]
        for bit in bits[:-1]:
            part = call(added_body, shape(part.shape, bf16), 2, traffic=6 * part.size)(
                part, passed(part, "expert", bit)
            )
        changed = call(
            changed_body, shape(chosen.shape, bf16), 3, traffic=8 * chosen.size, limit=2 * mib + 32 * chosen.size
        )(part, passed(part, "expert", bits[-1]), chosen)
        return exchanged(changed, "layer")

    def apply_limit(size, wanted):
        return 8 * mib + 16 * sections * wanted * width + 8 * size * width

    def applied(rows, sent, changed):
        size, wanted = rows.shape[0], changed[0].shape[0]
        return call(
            functools.partial(apply_body, sections),
            (shape(rows.shape, bf16), shape((1, 1), f32)),
            2 + sections,
            scalars=1,
            flops=2 * size * sections * wanted * width,
            traffic=4 * size * width,
            limit=apply_limit(size, wanted),
        )(layer, rows, sent, *changed)

    def passes(rows, count, weights):
        size = devices * count
        wanted = 2 * count
        part, chosen, sent = call(
            functools.partial(pass_body, count, flight),
            pass_shapes(size, wanted),
            5,
            scalars=1,
            flops=6 * wanted * width * units,
            traffic=2 * size * width,
            limit=pass_limit(size),
        )(member, rows, gain, *weights)
        return applied(rows, sent, summed(part, chosen))

    def finish(rows, count, weights, sent=None, changed=()):
        size = devices * count
        side = size // 2
        body = functools.partial(final_body, half, flight)
        operands = (member, rows)
        more_scratch = []
        if changed:
            body = functools.partial(changed_final_body, half, sections, flight)
            operands = (layer, member, rows, sent, *changed)
            more_scratch = [pltpu.VMEM(rows.shape, bf16), pltpu.VMEM((1, 1), f32)]
        hidden, raw, near, far = call(
            body,
            (
                shape((size, units), bf16),
                shape((count, width), bf16),
                shape((side, width), bf16),
                shape((side, width + 2 * units), bf16),
            ),
            5 + (1 + sections if changed else 0),
            scalars=2 if changed else 1,
            scratch=[pltpu.VMEM((devices, -(-count // 8) * 8, units), f32)] + more_scratch,
            flops=6 * size * width * units,
            traffic=6 * width * units,
            limit=8 * mib
            + 24 * min(size, CHUNK) * width
            + 4 * size * width
            + 16 * size * units
            + (apply_limit(size, changed[0].shape[0]) if changed else 0),
        )(*operands, gain, *weights)
        far = passed(far, "expert", 1)
        behind = 2 * devices * units
        sums = call(
            functools.partial(paired_body, half),
            tuple(
                shape((count, width + (behind if 0 < q < GROUP // 2 else 0)), bf16) for q in range(half)
            ),
            3,
            traffic=6 * side * width,
            limit=4 * mib + 20 * side * width + 24 * count * behind,
        )(near, far, hidden)
        arrived = [passed(sums[q], "expert", 2 * q) for q in range(half - 1, 0, -1)]
        arrived = [sums[0]] + arrived[::-1]
        fresh = call(
            functools.partial(combine_body, half),
            shape((count, width), bf16),
            half + 1,
            traffic=2 * side * width,
            limit=2 * mib + 16 * count * width + 6 * count * behind,
        )(*arrived, raw)
        blocks = exchanged(fresh, "layer")
        gram = call(
            functools.partial(gram_body, scale, width),
            shape((units, GROUP * units), f32),
            2 + GROUP // 2 - 1,
            scalars=1,
            scratch=[pltpu.VMEM((units, GROUP * units), f32), pltpu.SemaphoreType.DMA(())],
            placed=HBM,
            flops=2 * size * units * units * GROUP,
            traffic=4 * units * units * GROUP,
            limit=8 * mib + 64 * size * units,
        )(member, hidden, far, *arrived[1:GROUP // 2])
        new_state = call(
            functools.partial(merge_body, sections),
            shape((tokens, width), bf16),
            2 * sections + 1,
            scalars=1,
            scratch=[pltpu.VMEM((tokens, width), bf16), pltpu.SemaphoreType.DMA((chunks,))],
            placed=HBM,
            traffic=4 * tokens * width,
            limit=8 * mib + 16 * sections * count * width,
        )(layer, *blocks, *tables, state)
        return new_state, gram

    def looped(rows, more, count, weights):
        _, rows = lax.while_loop(
            lambda carry: carry[0][0, 0] > 0.5,
            lambda carry: passes(carry[1], count, weights)[::-1],
            (more, rows),
        )
        return finish(rows, count, weights)

    table, kept_routes = call(
        functools.partial(table_body, flight), (shape((1, tokens), bf16), shape(routes.shape, routes.dtype)), 1
    )(routes)
    tables = exchanged(table, "layer")
    raw = call(
        rows_body, shape((few, width), bf16), 2, traffic=2 * tokens * width, limit=8 * mib
    )(table, state)
    gate_weights = call(gates_body, shape((flight, tokens), f32), 2)(kept_routes, gates)
    payload = payload_of(few, raw, gate_weights)
    near = [payload] + [passed(payload, "expert", r) for r in range(2, devices, 2)]
    pair = passed(jnp.stack(near), "expert", 1)
    weights = call(
        held_body,
        tuple(shape(w.shape, bf16) for w in (w_gate, w_up, w_down)),
        1,
        streamed=3,
        scratch=[pltpu.SemaphoreType.DMA((3,))],
        traffic=12 * w_gate.size,
        limit=6 * w_gate.size + 2 * mib,
    )(near[1], w_gate, w_up, w_down)
    size = devices * few
    rows, mode, part, chosen, sent = call(
        functools.partial(first_pass_body, half, sections, few, flight),
        (shape((size, width + LANES), bf16), shape((1, 1), jnp.int32)) + pass_shapes(size, 2 * few),
        half + 5,
        scalars=1,
        flops=12 * few * width * units,
        traffic=4 * size * width,
        limit=pass_limit(size),
    )(member, *near, pair, gain, *weights)

    def once(share):
        def run(rows, part, chosen, sent, gate_weights, *weights):
            wanted = part.shape[0] // share
            return finish(rows, few, weights, sent, summed(part[:wanted], chosen[:wanted]))

        return run

    def again(rows, part, chosen, sent, gate_weights, *weights):
        rows, more = applied(rows, sent, summed(part, chosen))
        return looped(rows, more, few, weights)

    def filled(rows, part, chosen, sent, gate_weights, *weights):
        most = fronts * CAP * flight
        raw = call(
            rows_body, shape((most, width), bf16), 2, traffic=2 * tokens * width, limit=8 * mib
        )(table, state)
        payload = payload_of(most, raw, gate_weights)
        near = [payload] + [passed(payload, "expert", r) for r in range(2, devices, 2)]
        rows = call(
            functools.partial(stack_body, half),
            shape((devices * most, width + LANES), bf16),
            half + 1,
            traffic=4 * devices * most * width,
            limit=4 * mib + 16 * devices * most * width,
        )(*near, passed(jnp.stack(near), "expert", 1))
        return looped(rows, jnp.ones((1, 1), f32), most, weights)

    state, gram = lax.switch(
        mode[0, 0], (once(4), once(2), once(1), again, filled), rows, part, chosen, sent, gate_weights, *weights
    )
    return state.reshape(1, fronts, tok_rows, width), gram[None]


def solution(mesh):
    return jax.shard_map(
        shards,
        mesh=mesh,
        in_specs=(
            P(None, "expert", None),
            P("layer", None),
            P("layer", None, "expert"),
            P("layer", None, "expert"),
            P("layer", "expert", None),
            P("layer", None, "expert", None),
            P("layer", None, "expert", None),
        ),
        out_specs=(P("layer", None, "expert", None), P("layer", "expert", None)),
        check_vma=False,
    )
```

time: 280 us -> 64.3 us (0.23)
  starting transfers between devices: 129 us -> 23.9 us
  matrix products: 42.7 us -> 0 us
  waiting for transfers between devices: 63 us -> 21.3 us
  other arithmetic: 22.1 us -> 0.18 us
  local copies, waits for them, and re-layouts: 18.6 us -> 6.25 us
  Pallas kernels: 0 us -> 9.5 us
    ppermute x28 -> x20, starting transfers between devices: 79 us -> 23.9 us  [passed(): lax.ppermute(value, axis, [(i, i ^ r) for i in range(lax.axis_size(axis))])]
    all_to_all x14 -> x0, starting transfers between devices: 50.1 us -> none  [the longest x7 26.6 us: layer_step(): lax.all_to_all(outbound, 'expert', split_axis=0, concat_axis=0, tiled=True)]
    all_to_all x14 -> x0, waiting for transfers between devices: 42.7 us -> none  [the longest x7 42.3 us: layer_step(): lax.all_to_all(outbound, 'expert', split_axis=0, concat_axis=0, tiled=True)]
    dot_general x42 -> x0, matrix products: 42.7 us -> none  [the longest x7 13.9 us: layer_step(): gate_act = jnp.dot(rows, gate_weight, preferred_element_type=jnp.float32)]
    reduce_sum x21 -> x0, other arithmetic: 13.7 us -> none  [the longest x7 7.95 us: normalize(): scale = lax.rsqrt(jnp.mean(wide * wide, axis=-1, keepdims=True) + EPSILON)]
    reshape x21 -> x0, local copies, waits for them, and re-layouts: 10.2 us -> none  [the longest x7 4.99 us: layer_step(): jnp.broadcast_to(outbound[:, None], (flight, GROUP, CAP, width))]
    pallas_call x0 -> x14, Pallas kernels: none -> 9.5 us  [the longest x1 1.81 us: finish(): call(functools.partial(gram_body, scale, width), shape((units, GROUP * un...]
    dynamic_slice x7 -> x0, local copies, waits for them, and re-layouts: 6.67 us -> none  [advance(): kept = lax.dynamic_index_in_dim(produced, slot, 0, keepdims=False)]
  transfers between devices with their start and end apart: 42 -> 20, of which waited for: 23 -> 11; matrix products, arithmetic and copies ran while one was open for 10% -> 0% of each run, Pallas kernels for 0% -> 6%
where the time goes in v1:
time: 64.3 us; the launch traced here: 63.1 us
  starting transfers between devices  23.9 us (37%)
  waiting for transfers between devices  21.3 us (33%)
  Pallas kernels  9.5 us (15%)
  local copies, waits for them, and re-layouts  6.25 us (10%)
  between operations  1.53 us (2%)
    ppermute x20, starting transfers between devices, passed(): lax.ppermute(value, axis, [(i, i ^ r) for i in range(lax.axis_size(axis))])  23.9 us
    ppermute x20, waiting for transfers between devices, passed(): lax.ppermute(value, axis, [(i, i ^ r) for i in range(lax.axis_size(axis))])  21.3 us
    unnamed x14, local copies, waits for them, and re-layouts  6.23 us
    pallas_call x1, Pallas kernels, finish(): call(functools.partial(gram_body, scale, width), shape((units, GROUP * un...  1.81 us
    pallas_call x1, Pallas kernels, shards(): call(functools.partial(first_pass_body, half, sections, few, flight), (sh...  1.71 us
    pallas_call x1, Pallas kernels, finish(): call(body, (shape((size, units), bf16), shape((count, width), bf16), shap...  1.55 us
    pallas_call x1, Pallas kernels, shards(): call(rows_body, shape((few, width), bf16), 2, traffic=2 * tokens * width,...  1.51 us
    pallas_call x1, Pallas kernels, finish(): call(functools.partial(merge_body, sections), shape((tokens, width), bf16...  1.43 us
  transfers between devices with their start and end apart: 20, of which 11 were waited for; matrix products, arithmetic and copies ran while one was open for 0% of the time, Pallas kernels for 6%

profile of v1, /device:TPU:1, one launch (start us, length us, event | category | flops | bytes accessed | tf_op | source)
XLA Modules:
  0.0 63.1 jit_solution(17278935653796016019)
XLA Ops:
  0.6 0.7 %copy-done.3 = s32[1,4,32,8]{2,3,1,0:T(8,128)S(1)} copy-done((s32[1,4,32,8]{2,3,1,0:T(8,128)S(1)}, s32[1,4,32,8]{2,3,1,0:T(8,128)}, u32[]{:S(2)}) %copy-start.3) | copy-done | bytes 4120
  1.3 0.1 shard_map.96
  1.4 2.6 %collective-permute-start.77 = (bf16[1,128]{1,0:T(2,128)(2,1)S(1)}, bf16[1,128]{1,0:T(2,128)(2,1)S(1)}, u32[]{:S(2)}, u32[]{:S(2)}) collective-permute-start(bf16[1,128]{1,0:T(2,128)(2,1)S(1)} %get-tuple-element.367.table_ref.refs_0_), channel_id=1, source_target_pairs={{0,24},{8,16},{16,8},{24,0},{1,25},{9,17},{17,9},{25,1},{2,26},{10... | collective-permute-start | bytes 776 | tf_op jit(solution)/shard_map/ppermute | solution.py:450
  4.1 0.5 collective-permute-start.75
  4.5 0.1 pad_add_fusion.index_ref
  4.6 1.5 %shard_map.98.refs_5_ = bf16[4,3584]{1,0:T(4,128)(2,1)S(1)} custom-call(bf16[1,128]{1,0:T(2,128)(2,1)S(1)} %get-tuple-element.367.table_ref.refs_0_, bf16[128,3584]{1,0:T(8,128)(2,1)} %bitcast.46), custom_call_target="tpu_custom_call" | custom-call | bytes 917504 | tf_op jit(solution)/shard_map/pallas_call | solution.py:622
  6.1 0.0 copy-start.4
  6.1 0.7 %copy-done.4 = f32[1,4,32,8]{2,3,1,0:T(8,128)S(1)} copy-done((f32[1,4,32,8]{2,3,1,0:T(8,128)S(1)}, f32[1,4,32,8]{2,3,1,0:T(8,128)}, u32[]{:S(2)}) %copy-start.4) | copy-done | bytes 4120
  6.9 0.1 shard_map.97.refs_4_
  7.0 0.8 %shard_map.99.refs_0_ = bf16[4,3712]{1,0:T(4,128)(2,1)S(1)} custom-call(s32[2]{0:T(128)S(1)} %pad_add_fusion.index_ref, bf16[1,128]{1,0:T(2,128)(2,1)S(1)} %get-tuple-element.367.table_ref.refs_0_, bf16[1,128]{1,0:T(2,128)(2,1)S(1)} %collective-permute-done.75.refs_1_, bf16[1,128]{1,0:T(2,128)(2,1)S(1)} %collective-permute-done.76.refs_2_, ...), custom_call_target="tpu_custom_call" | custom-call | tf_op jit(solution)/shard_map/pallas_call | solution.py:479
  7.8 3.3 %collective-permute-start.80 = (bf16[4,3712]{1,0:T(4,128)(2,1)S(1)}, bf16[4,3712]{1,0:T(4,128)(2,1)S(1)}, u32[]{:S(2)}, u32[]{:S(2)}) collective-permute-start(bf16[4,3712]{1,0:T(4,128)(2,1)S(1)} %shard_map.99.refs_0_), channel_id=1, source_target_pairs={{0,6},{1,7},{2,4},{3,5},{4,2},{5,3},{6,0},{7,1},{8,14},{9,15},{10,... | collective-permute-start | bytes 89096 | tf_op jit(solution)/shard_map/ppermute | solution.py:450
  11.1 0.3 collective-permute-start.78
  11.4 1.0 %collective-permute-done.80.refs_3_ = bf16[4,3712]{1,0:T(4,128)(2,1)S(1)} collective-permute-done((bf16[4,3712]{1,0:T(4,128)(2,1)S(1)}, bf16[4,3712]{1,0:T(4,128)(2,1)S(1)}, u32[]{:S(2)}, u32[]{:S(2)}) %collective-permute-start.80) | collective-permute-done | bytes 29728 | tf_op jit(solution)/shard_map/ppermute | solution.py:450
  12.4 2.7 %collective-permute-done.79.refs_2_ = bf16[4,3712]{1,0:T(4,128)(2,1)S(1)} collective-permute-done((bf16[4,3712]{1,0:T(4,128)(2,1)S(1)}, bf16[4,3712]{1,0:T(4,128)(2,1)S(1)}, u32[]{:S(2)}, u32[]{:S(2)}) %collective-permute-start.79) | collective-permute-done | bytes 29728 | tf_op jit(solution)/shard_map/ppermute | solution.py:450
  15.0 0.1 pad_maximum_fusion.1
  15.2 1.3 %collective-permute-start.81 = (bf16[4,4,3712]{2,1,0:T(4,128)(2,1)S(1)}, bf16[4,4,3712]{2,1,0:T(4,128)(2,1)S(1)}, u32[]{:S(2)}, u32[]{:S(2)}) collective-permute-start(bf16[4,4,3712]{2,1,0:T(4,128)(2,1)S(1)} %pad_maximum_fusion.1), channel_id=1, source_target_pairs={{0,1},{1,0},{2,3},{3,2},{4,5},{5,4},{6,7},{7,6},{8,9},{9,8},{10,11... | collective-permute-start | bytes 356360 | tf_op jit(solution)/shard_map/ppermute | solution.py:450
  16.4 1.5 %copy-done = bf16[1,3584,256]{2,1,0:T(8,128)(2,1)S(1)} copy-done((bf16[1,3584,256]{2,1,0:T(8,128)(2,1)S(1)}, bf16[1,3584,256]{2,1,0:T(8,128)(2,1)}, u32[]{:S(2)}) %copy-start) | copy-done | bytes 1835032
  17.9 1.5 %copy-done.1 = bf16[1,3584,256]{2,1,0:T(8,128)(2,1)S(1)} copy-done((bf16[1,3584,256]{2,1,0:T(8,128)(2,1)S(1)}, bf16[1,3584,256]{2,1,0:T(8,128)(2,1)}, u32[]{:S(2)}) %copy-start.1) | copy-done | bytes 1835032
  19.4 1.5 %copy-done.2 = bf16[1,256,3584]{2,1,0:T(8,128)(2,1)S(1)} copy-done((bf16[1,256,3584]{2,1,0:T(8,128)(2,1)S(1)}, bf16[1,256,3584]{2,1,0:T(8,128)(2,1)}, u32[]{:S(2)}) %copy-start.2) | copy-done | bytes 1835032
  20.9 0.4 shard_map.100
  21.4 0.3 copy-done.6
  21.6 1.7 %shard_map.101 = (bf16[32,3712]{1,0:T(8,128)(2,1)S(1)}, s32[1,1]{1,0:T(1,128)}, bf16[8,3584]{1,0:T(8,128)(2,1)S(1)}, bf16[8,3712]{1,0:T(8,128)(2,1)S(1)}, f32[1,32]{1,0:T(1,128)S(1)}) custom-call(s32[1]{0:T(128)} %bitcast.16.member_ref, bf16[4,3712]{1,0:T(4,128)(2,1)S(1)} %shard_map.99.refs_0_, ...), custom_call_target="tpu_custom_call" | custom-call | flops 44040192 | bytes 458752 | tf_op jit(solution)/shard_map/pallas_call | solution.py:639
  24.0 38.9 %conditional.1 = (bf16[1,4,32,3584]{3,2,1,0:T(8,128)(2,1)}, f32[1,256,2048]{2,1,0:T(8,128)}) conditional(s32[]{:T(128)} %bitcast.30, (bf16[8,3584]{1,0:T(8,128)(2,1)S(1)}, bf16[8,3712]{1,0:T(8,128)(2,1)S(1)}, s32[1]{0:T(128)}, s32[1]{0:T(128)}, bf16[32,3712]{1,0:T(8,128)(2,1)S(1)}, /*index=5*/f32[1,32]{1,0:T(1,128)S(1)}, ...), branch_computations={%region_0.0_spmd, %region_1.0_spmd, %region_2.0_spmd, %region_3.0_... | conditional | flops 537227264 | bytes 23831368 | solution.py:676
  24.0 0.3 collective-permute-start
  24.4 2.3 %collective-permute-done.b_ref = bf16[2,3584]{1,0:T(2,128)(2,1)S(1)} collective-permute-done((bf16[2,3584]{1,0:T(2,128)(2,1)S(1)}, bf16[2,3584]{1,0:T(2,128)(2,1)S(1)}, u32[]{:S(2)}, u32[]{:S(2)}) %collective-permute-start) | collective-permute-done | bytes 14368 | tf_op jit(solution)/shard_map/cond/branch_0_fun/ppermute | solution.py:450
  26.7 0.1 collective-permute-start.1
  26.8 2.6 %collective-permute-done.1.b_ref = bf16[2,3584]{1,0:T(2,128)(2,1)S(1)} collective-permute-done((bf16[2,3584]{1,0:T(2,128)(2,1)S(1)}, bf16[2,3584]{1,0:T(2,128)(2,1)S(1)}, u32[]{:S(2)}, u32[]{:S(2)}) %collective-permute-start.1) | collective-permute-done | bytes 14368 | tf_op jit(solution)/shard_map/cond/branch_0_fun/ppermute | solution.py:450
  29.4 1.3 %collective-permute-start.2 = (bf16[2,3584]{1,0:T(2,128)(2,1)S(1)}, bf16[2,3584]{1,0:T(2,128)(2,1)S(1)}, u32[]{:S(2)}, u32[]{:S(2)}) collective-permute-start(bf16[2,3584]{1,0:T(2,128)(2,1)S(1)} %branch_0_fun.9.a_ref), channel_id=1, source_target_pairs={{0,4},{1,5},{2,6},{3,7},{4,0},{5,1},{6,2},{7,3},{8,12},{9,13},{10,... | collective-permute-start | bytes 43016 | tf_op jit(solution)/shard_map/cond/branch_0_fun/ppermute | solution.py:450
  30.7 2.3 %collective-permute-done.2.b_ref = bf16[2,3584]{1,0:T(2,128)(2,1)S(1)} collective-permute-done((bf16[2,3584]{1,0:T(2,128)(2,1)S(1)}, bf16[2,3584]{1,0:T(2,128)(2,1)S(1)}, u32[]{:S(2)}, u32[]{:S(2)}) %collective-permute-start.2) | collective-permute-done | bytes 14368 | tf_op jit(solution)/shard_map/cond/branch_0_fun/ppermute | solution.py:450
  33.0 6.2 %collective-permute-start.5 = (bf16[2,3712]{1,0:T(2,128)(2,1)S(1)}, bf16[2,3712]{1,0:T(2,128)(2,1)S(1)}, u32[]{:S(2)}, u32[]{:S(2)}) collective-permute-start(bf16[2,3712]{1,0:T(2,128)(2,1)S(1)} %branch_0_fun.10.refs_0_), channel_id=1, source_target_pairs={{0,24},{8,16},{16,8},{24,0},{1,25},{9,17},{17,9},{25,1},{2,26},{10... | collective-permute-start | bytes 44552 | tf_op jit(solution)/shard_map/cond/branch_0_fun/ppermute | solution.py:450
  39.2 0.5 collective-permute-start.4
  39.7 0.0 collective-permute-start.3
  39.7 0.9 %collective-permute-done.5.refs_3_ = bf16[2,3712]{1,0:T(2,128)(2,1)S(1)} collective-permute-done((bf16[2,3712]{1,0:T(2,128)(2,1)S(1)}, bf16[2,3712]{1,0:T(2,128)(2,1)S(1)}, u32[]{:S(2)}, u32[]{:S(2)}) %collective-permute-start.5) | collective-permute-done | bytes 14880 | tf_op jit(solution)/shard_map/cond/branch_0_fun/ppermute | solution.py:450
  40.6 1.2 %collective-permute-done.4.refs_2_ = bf16[2,3712]{1,0:T(2,128)(2,1)S(1)} collective-permute-done((bf16[2,3712]{1,0:T(2,128)(2,1)S(1)}, bf16[2,3712]{1,0:T(2,128)(2,1)S(1)}, u32[]{:S(2)}, u32[]{:S(2)}) %collective-permute-start.4) | collective-permute-done | bytes 14880 | tf_op jit(solution)/shard_map/cond/branch_0_fun/ppermute | solution.py:450
  41.8 1.5 %branch_0_fun.11 = (bf16[32,256]{1,0:T(8,128)(2,1)S(1)}, bf16[4,3584]{1,0:T(4,128)(2,1)S(1)}, bf16[16,3584]{1,0:T(8,128)(2,1)S(1)}, bf16[16,4096]{1,0:T(8,128)(2,1)S(1)}) custom-call(s32[1]{0:T(128)} %get-tuple-element.212.layer_ref, s32[1]{0:T(128)} %get-tuple-element.213.member_ref, bf16[32,3712]{1,0:T(8,128)(2,1)S(1)} %get-tuple-element.214.rows_ref, ...), custom_call_target="tpu_custom_call" | custom-call | flops 176160768 | bytes 5505024 | tf_op jit(solution)/shard_map/cond/branch_0_fun/pallas_call | solution.py:547
  43.3 0.3 collective-permute-start.6
  43.7 4.5 %collective-permute-done.6.far_ref = bf16[16,4096]{1,0:T(8,128)(2,1)S(1)} collective-permute-done((bf16[16,4096]{1,0:T(8,128)(2,1)S(1)}, bf16[16,4096]{1,0:T(8,128)(2,1)S(1)}, u32[]{:S(2)}, u32[]{:S(2)}) %collective-permute-start.6) | collective-permute-done | bytes 131104 | tf_op jit(solution)/shard_map/cond/branch_0_fun/ppermute | solution.py:450
  48.2 0.1 branch_0_fun.12
  48.2 0.1 collective-permute-start.7
  48.3 1.8 %collective-permute-start.8 = (bf16[4,7680]{1,0:T(4,128)(2,1)S(1)}, bf16[4,7680]{1,0:T(4,128)(2,1)S(1)}, u32[]{:S(2)}, u32[]{:S(2)}) collective-permute-start(bf16[4,7680]{1,0:T(4,128)(2,1)S(1)} %get-tuple-element.227), channel_id=1, source_target_pairs={{0,4},{1,5},{2,6},{3,7},{4,0},{5,1},{6,2},{7,3},{8,12},{9,13},{10,... | collective-permute-start | bytes 184328 | tf_op jit(solution)/shard_map/cond/branch_0_fun/ppermute | solution.py:450
  50.1 1.7 %collective-permute-start.9 = (bf16[4,7680]{1,0:T(4,128)(2,1)S(1)}, bf16[4,7680]{1,0:T(4,128)(2,1)S(1)}, u32[]{:S(2)}, u32[]{:S(2)}) collective-permute-start(bf16[4,7680]{1,0:T(4,128)(2,1)S(1)} %get-tuple-element.228), channel_id=1, source_target_pairs={{0,6},{1,7},{2,4},{3,5},{4,2},{5,3},{6,0},{7,1},{8,14},{9,15},{10,... | collective-permute-start | bytes 184328 | tf_op jit(solution)/shard_map/cond/branch_0_fun/ppermute | solution.py:450
  51.8 0.5 collective-permute-done.8.refs_2_.refs_1_
  52.3 3.2 %collective-permute-done.9.refs_3_.refs_2_ = bf16[4,7680]{1,0:T(4,128)(2,1)S(1)} collective-permute-done((bf16[4,7680]{1,0:T(4,128)(2,1)S(1)}, bf16[4,7680]{1,0:T(4,128)(2,1)S(1)}, u32[]{:S(2)}, u32[]{:S(2)}) %collective-permute-start.9) | collective-permute-done | bytes 61472 | tf_op jit(solution)/shard_map/cond/branch_0_fun/ppermute | solution.py:450
  55.5 2.6 %collective-permute-start.12 = (bf16[4,3584]{1,0:T(4,128)(2,1)S(1)}, bf16[4,3584]{1,0:T(4,128)(2,1)S(1)}, u32[]{:S(2)}, u32[]{:S(2)}) collective-permute-start(bf16[4,3584]{1,0:T(4,128)(2,1)S(1)} %branch_0_fun.13.refs_0_), channel_id=1, source_target_pairs={{0,24},{8,16},{16,8},{24,0},{1,25},{9,17},{17,9},{25,1},{2,26},{10... | collective-permute-start | bytes 86024 | tf_op jit(solution)/shard_map/cond/branch_0_fun/ppermute | solution.py:450
  58.1 1.0 %collective-permute-start.11 = (bf16[4,3584]{1,0:T(4,128)(2,1)S(1)}, bf16[4,3584]{1,0:T(4,128)(2,1)S(1)}, u32[]{:S(2)}, u32[]{:S(2)}) collective-permute-start(bf16[4,3584]{1,0:T(4,128)(2,1)S(1)} %branch_0_fun.13.refs_0_), channel_id=1, source_target_pairs={{0,16},{8,24},{16,0},{24,8},{1,17},{9,25},{17,1},{25,9},{2,18},{10... | collective-permute-start | bytes 86024 | tf_op jit(solution)/shard_map/cond/branch_0_fun/ppermute | solution.py:450
  59.1 1.8 %branch_0_fun.15 = f32[256,2048]{1,0:T(8,128)} custom-call(s32[1]{0:T(128)} %get-tuple-element.213.member_ref, bf16[32,256]{1,0:T(8,128)(2,1)S(1)} %get-tuple-element.224.hidden_ref.mine_ref, bf16[16,4096]{1,0:T(8,128)(2,1)S(1)} %collective-permute-done.6.far_ref, bf16[4,7680]{1,0:T(4,128)(2,1)S(1)} %collective-permute-done.7.refs_1_.refs_0_, ...), custom_call_target="tpu_custom_call" | custom-call | flops 33554432 | bytes 2097152 | tf_op jit(solution)/shard_map/cond/branch_0_fun/pallas_call | solution.py:587
  60.9 0.3 collective-permute-done.11.refs_2_
  61.2 1.4 %branch_0_fun.14 = bf16[128,3584]{1,0:T(8,128)(2,1)} custom-call(s32[1]{0:T(128)} %get-tuple-element.212.layer_ref, bf16[4,3584]{1,0:T(4,128)(2,1)S(1)} %branch_0_fun.13.refs_0_, bf16[4,3584]{1,0:T(4,128)(2,1)S(1)} %collective-permute-done.10.refs_1_, bf16[4,3584]{1,0:T(4,128)(2,1)S(1)} %collective-permute-done.11.refs_2_, ...), custom_call_target="tpu_custom_call" | custom-call | bytes 1835008 | tf_op jit(solution)/shard_map/cond/branch_0_fun/pallas_call | solution.py:598
  (25 shorter events, 0.2 us)
Async XLA Ops:
  0.6 0.7 %copy-start.3 = (s32[1,4,32,8]{2,3,1,0:T(8,128)S(1)}, s32[1,4,32,8]{2,3,1,0:T(8,128)}, u32[]{:S(2)}) copy-start(s32[1,4,32,8]{2,3,1,0:T(8,128)} %param.21) | copy-start | bytes 12292
  1.4 5.5 %collective-permute-start.77 = (bf16[1,128]{1,0:T(2,128)(2,1)S(1)}, bf16[1,128]{1,0:T(2,128)(2,1)S(1)}, u32[]{:S(2)}, u32[]{:S(2)}) collective-permute-start(bf16[1,128]{1,0:T(2,128)(2,1)S(1)} %get-tuple-element.367.table_ref.refs_0_), channel_id=1, source_target_pairs={{0,24},{8,16},{16,8},{24,0},{1,25},{9,17},{17,9},{25,1},{2,26},{10... | collective-permute-start | bytes 776 | tf_op jit(solution)/shard_map/ppermute | solution.py:450
  4.1 2.9 %collective-permute-start.76 = (bf16[1,128]{1,0:T(2,128)(2,1)S(1)}, bf16[1,128]{1,0:T(2,128)(2,1)S(1)}, u32[]{:S(2)}, u32[]{:S(2)}) collective-permute-start(bf16[1,128]{1,0:T(2,128)(2,1)S(1)} %get-tuple-element.367.table_ref.refs_0_), channel_id=1, source_target_pairs={{0,16},{8,24},{16,0},{24,8},{1,17},{9,25},{17,1},{25,9},{2,18},{10... | collective-permute-start | bytes 776 | tf_op jit(solution)/shard_map/ppermute | solution.py:450
  4.1 2.9 %collective-permute-start.75 = (bf16[1,128]{1,0:T(2,128)(2,1)S(1)}, bf16[1,128]{1,0:T(2,128)(2,1)S(1)}, u32[]{:S(2)}, u32[]{:S(2)}) collective-permute-start(bf16[1,128]{1,0:T(2,128)(2,1)S(1)} %get-tuple-element.367.table_ref.refs_0_), channel_id=1, source_target_pairs={{0,8},{8,0},{16,24},{24,16},{1,9},{9,1},{17,25},{25,17},{2,10},{10... | collective-permute-start | bytes 776 | tf_op jit(solution)/shard_map/ppermute | solution.py:450
  6.1 0.7 %copy-start.4 = (f32[1,4,32,8]{2,3,1,0:T(8,128)S(1)}, f32[1,4,32,8]{2,3,1,0:T(8,128)}, u32[]{:S(2)}) copy-start(f32[1,4,32,8]{2,3,1,0:T(8,128)} %param.22) | copy-start | bytes 12292
  7.8 4.6 %collective-permute-start.80 = (bf16[4,3712]{1,0:T(4,128)(2,1)S(1)}, bf16[4,3712]{1,0:T(4,128)(2,1)S(1)}, u32[]{:S(2)}, u32[]{:S(2)}) collective-permute-start(bf16[4,3712]{1,0:T(4,128)(2,1)S(1)} %shard_map.99.refs_0_), channel_id=1, source_target_pairs={{0,6},{1,7},{2,4},{3,5},{4,2},{5,3},{6,0},{7,1},{8,14},{9,15},{10,... | collective-permute-start | bytes 89096 | tf_op jit(solution)/shard_map/ppermute | solution.py:450
  11.1 4.0 %collective-permute-start.79 = (bf16[4,3712]{1,0:T(4,128)(2,1)S(1)}, bf16[4,3712]{1,0:T(4,128)(2,1)S(1)}, u32[]{:S(2)}, u32[]{:S(2)}) collective-permute-start(bf16[4,3712]{1,0:T(4,128)(2,1)S(1)} %shard_map.99.refs_0_), channel_id=1, source_target_pairs={{0,4},{1,5},{2,6},{3,7},{4,0},{5,1},{6,2},{7,3},{8,12},{9,13},{10,... | collective-permute-start | bytes 89096 | tf_op jit(solution)/shard_map/ppermute | solution.py:450
  11.1 4.0 %collective-permute-start.78 = (bf16[4,3712]{1,0:T(4,128)(2,1)S(1)}, bf16[4,3712]{1,0:T(4,128)(2,1)S(1)}, u32[]{:S(2)}, u32[]{:S(2)}) collective-permute-start(bf16[4,3712]{1,0:T(4,128)(2,1)S(1)} %shard_map.99.refs_0_), channel_id=1, source_target_pairs={{0,2},{1,3},{2,0},{3,1},{4,6},{5,7},{6,4},{7,5},{8,10},{9,11},{10,... | collective-permute-start | bytes 89096 | tf_op jit(solution)/shard_map/ppermute | solution.py:450
  15.2 6.2 %collective-permute-start.81 = (bf16[4,4,3712]{2,1,0:T(4,128)(2,1)S(1)}, bf16[4,4,3712]{2,1,0:T(4,128)(2,1)S(1)}, u32[]{:S(2)}, u32[]{:S(2)}) collective-permute-start(bf16[4,4,3712]{2,1,0:T(4,128)(2,1)S(1)} %pad_maximum_fusion.1), channel_id=1, source_target_pairs={{0,1},{1,0},{2,3},{3,2},{4,5},{5,4},{6,7},{7,6},{8,9},{9,8},{10,11... | collective-permute-start | bytes 356360 | tf_op jit(solution)/shard_map/ppermute | solution.py:450
  16.4 1.5 %copy-start = (bf16[1,3584,256]{2,1,0:T(8,128)(2,1)S(1)}, bf16[1,3584,256]{2,1,0:T(8,128)(2,1)}, u32[]{:S(2)}) copy-start(bf16[1,3584,256]{2,1,0:T(8,128)(2,1)} %param.18) | copy-start | bytes 5505028
  17.9 1.5 %copy-start.1 = (bf16[1,3584,256]{2,1,0:T(8,128)(2,1)S(1)}, bf16[1,3584,256]{2,1,0:T(8,128)(2,1)}, u32[]{:S(2)}) copy-start(bf16[1,3584,256]{2,1,0:T(8,128)(2,1)} %param.19) | copy-start | bytes 5505028
  19.4 1.5 %copy-start.2 = (bf16[1,256,3584]{2,1,0:T(8,128)(2,1)S(1)}, bf16[1,256,3584]{2,1,0:T(8,128)(2,1)}, u32[]{:S(2)}) copy-start(bf16[1,256,3584]{2,1,0:T(8,128)(2,1)} %param.20) | copy-start | bytes 5505028
  20.9 0.7 %copy-start.6 = (f32[1,3584]{1,0:T(1,128)S(1)}, f32[1,3584]{1,0:T(1,128)}, u32[]{:S(2)}) copy-start(f32[1,3584]{1,0:T(1,128)} %refs_5_.1) | copy-start | bytes 43012
  21.3 2.7 %copy-start.5 = (bf16[4,32,3584]{2,1,0:T(8,128)(2,1)S(1)}, bf16[4,32,3584]{2,1,0:T(8,128)(2,1)}, u32[]{:S(2)}) copy-start(bf16[4,32,3584]{2,1,0:T(8,128)(2,1)} %param.16) | copy-start | bytes 2752516
  24.0 2.6 %collective-permute-start = (bf16[2,3584]{1,0:T(2,128)(2,1)S(1)}, bf16[2,3584]{1,0:T(2,128)(2,1)S(1)}, u32[]{:S(2)}, u32[]{:S(2)}) collective-permute-start(bf16[2,3584]{1,0:T(2,128)(2,1)S(1)} %slice.8.a_ref), channel_id=1, source_target_pairs={{0,1},{1,0},{2,3},{3,2},{4,5},{5,4},{6,7},{7,6},{8,9},{9,8},{10,11... | collective-permute-start | bytes 43016 | tf_op jit(solution)/shard_map/cond/branch_0_fun/ppermute | solution.py:450
  26.7 2.6 %collective-permute-start.1 = (bf16[2,3584]{1,0:T(2,128)(2,1)S(1)}, bf16[2,3584]{1,0:T(2,128)(2,1)S(1)}, u32[]{:S(2)}, u32[]{:S(2)}) collective-permute-start(bf16[2,3584]{1,0:T(2,128)(2,1)S(1)} %branch_0_fun.8.a_ref), channel_id=1, source_target_pairs={{0,2},{1,3},{2,0},{3,1},{4,6},{5,7},{6,4},{7,5},{8,10},{9,11},{10,... | collective-permute-start | bytes 43016 | tf_op jit(solution)/shard_map/cond/branch_0_fun/ppermute | solution.py:450
  29.4 3.6 %collective-permute-start.2 = (bf16[2,3584]{1,0:T(2,128)(2,1)S(1)}, bf16[2,3584]{1,0:T(2,128)(2,1)S(1)}, u32[]{:S(2)}, u32[]{:S(2)}) collective-permute-start(bf16[2,3584]{1,0:T(2,128)(2,1)S(1)} %branch_0_fun.9.a_ref), channel_id=1, source_target_pairs={{0,4},{1,5},{2,6},{3,7},{4,0},{5,1},{6,2},{7,3},{8,12},{9,13},{10,... | collective-permute-start | bytes 43016 | tf_op jit(solution)/shard_map/cond/branch_0_fun/ppermute | solution.py:450
  33.0 7.6 %collective-permute-start.5 = (bf16[2,3712]{1,0:T(2,128)(2,1)S(1)}, bf16[2,3712]{1,0:T(2,128)(2,1)S(1)}, u32[]{:S(2)}, u32[]{:S(2)}) collective-permute-start(bf16[2,3712]{1,0:T(2,128)(2,1)S(1)} %branch_0_fun.10.refs_0_), channel_id=1, source_target_pairs={{0,24},{8,16},{16,8},{24,0},{1,25},{9,17},{17,9},{25,1},{2,26},{10... | collective-permute-start | bytes 44552 | tf_op jit(solution)/shard_map/cond/branch_0_fun/ppermute | solution.py:450
  39.2 2.6 %collective-permute-start.4 = (bf16[2,3712]{1,0:T(2,128)(2,1)S(1)}, bf16[2,3712]{1,0:T(2,128)(2,1)S(1)}, u32[]{:S(2)}, u32[]{:S(2)}) collective-permute-start(bf16[2,3712]{1,0:T(2,128)(2,1)S(1)} %branch_0_fun.10.refs_0_), channel_id=1, source_target_pairs={{0,16},{8,24},{16,0},{24,8},{1,17},{9,25},{17,1},{25,9},{2,18},{10... | collective-permute-start | bytes 44552 | tf_op jit(solution)/shard_map/cond/branch_0_fun/ppermute | solution.py:450
  39.7 2.1 %collective-permute-start.3 = (bf16[2,3712]{1,0:T(2,128)(2,1)S(1)}, bf16[2,3712]{1,0:T(2,128)(2,1)S(1)}, u32[]{:S(2)}, u32[]{:S(2)}) collective-permute-start(bf16[2,3712]{1,0:T(2,128)(2,1)S(1)} %branch_0_fun.10.refs_0_), channel_id=1, source_target_pairs={{0,8},{8,0},{16,24},{24,16},{1,9},{9,1},{17,25},{25,17},{2,10},{10... | collective-permute-start | bytes 44552 | tf_op jit(solution)/shard_map/cond/branch_0_fun/ppermute | solution.py:450
  43.3 4.8 %collective-permute-start.6 = (bf16[16,4096]{1,0:T(8,128)(2,1)S(1)}, bf16[16,4096]{1,0:T(8,128)(2,1)S(1)}, u32[]{:S(2)}, u32[]{:S(2)}) collective-permute-start(bf16[16,4096]{1,0:T(8,128)(2,1)S(1)} %get-tuple-element.223), channel_id=1, source_target_pairs={{0,1},{1,0},{2,3},{3,2},{4,5},{5,4},{6,7},{7,6},{8,9},{9,8},{10,11... | collective-permute-start | bytes 393224 | tf_op jit(solution)/shard_map/cond/branch_0_fun/ppermute | solution.py:450
  48.2 3.6 %collective-permute-start.7 = (bf16[4,7680]{1,0:T(4,128)(2,1)S(1)}, bf16[4,7680]{1,0:T(4,128)(2,1)S(1)}, u32[]{:S(2)}, u32[]{:S(2)}) collective-permute-start(bf16[4,7680]{1,0:T(4,128)(2,1)S(1)} %get-tuple-element.226), channel_id=1, source_target_pairs={{0,2},{1,3},{2,0},{3,1},{4,6},{5,7},{6,4},{7,5},{8,10},{9,11},{10,... | collective-permute-start | bytes 184328 | tf_op jit(solution)/shard_map/cond/branch_0_fun/ppermute | solution.py:450
  48.3 4.0 %collective-permute-start.8 = (bf16[4,7680]{1,0:T(4,128)(2,1)S(1)}, bf16[4,7680]{1,0:T(4,128)(2,1)S(1)}, u32[]{:S(2)}, u32[]{:S(2)}) collective-permute-start(bf16[4,7680]{1,0:T(4,128)(2,1)S(1)} %get-tuple-element.227), channel_id=1, source_target_pairs={{0,4},{1,5},{2,6},{3,7},{4,0},{5,1},{6,2},{7,3},{8,12},{9,13},{10,... | collective-permute-start | bytes 184328 | tf_op jit(solution)/shard_map/cond/branch_0_fun/ppermute | solution.py:450
  50.1 5.4 %collective-permute-start.9 = (bf16[4,7680]{1,0:T(4,128)(2,1)S(1)}, bf16[4,7680]{1,0:T(4,128)(2,1)S(1)}, u32[]{:S(2)}, u32[]{:S(2)}) collective-permute-start(bf16[4,7680]{1,0:T(4,128)(2,1)S(1)} %get-tuple-element.228), channel_id=1, source_target_pairs={{0,6},{1,7},{2,4},{3,5},{4,2},{5,3},{6,0},{7,1},{8,14},{9,15},{10,... | collective-permute-start | bytes 184328 | tf_op jit(solution)/shard_map/cond/branch_0_fun/ppermute | solution.py:450
  55.5 5.4 %collective-permute-start.12 = (bf16[4,3584]{1,0:T(4,128)(2,1)S(1)}, bf16[4,3584]{1,0:T(4,128)(2,1)S(1)}, u32[]{:S(2)}, u32[]{:S(2)}) collective-permute-start(bf16[4,3584]{1,0:T(4,128)(2,1)S(1)} %branch_0_fun.13.refs_0_), channel_id=1, source_target_pairs={{0,24},{8,16},{16,8},{24,0},{1,25},{9,17},{17,9},{25,1},{2,26},{10... | collective-permute-start | bytes 86024 | tf_op jit(solution)/shard_map/cond/branch_0_fun/ppermute | solution.py:450
  58.1 3.1 %collective-permute-start.11 = (bf16[4,3584]{1,0:T(4,128)(2,1)S(1)}, bf16[4,3584]{1,0:T(4,128)(2,1)S(1)}, u32[]{:S(2)}, u32[]{:S(2)}) collective-permute-start(bf16[4,3584]{1,0:T(4,128)(2,1)S(1)} %branch_0_fun.13.refs_0_), channel_id=1, source_target_pairs={{0,16},{8,24},{16,0},{24,8},{1,17},{9,25},{17,1},{25,9},{2,18},{10... | collective-permute-start | bytes 86024 | tf_op jit(solution)/shard_map/cond/branch_0_fun/ppermute | solution.py:450
  59.1 2.1 %collective-permute-start.10 = (bf16[4,3584]{1,0:T(4,128)(2,1)S(1)}, bf16[4,3584]{1,0:T(4,128)(2,1)S(1)}, u32[]{:S(2)}, u32[]{:S(2)}) collective-permute-start(bf16[4,3584]{1,0:T(4,128)(2,1)S(1)} %branch_0_fun.13.refs_0_), channel_id=1, source_target_pairs={{0,8},{8,0},{16,24},{24,16},{1,9},{9,1},{17,25},{25,17},{2,10},{10... | collective-permute-start | bytes 86024 | tf_op jit(solution)/shard_map/cond/branch_0_fun/ppermute | solution.py:450

commit v2 on v1

--- a/solution.py
+++ b/solution.py
@@ -15,7 +15,9 @@
 
 FEW = 4
 
-STATUS, SOURCE_LAYER, SOURCE_SLOT, WANTED, FULL, DEEP, DEVICE, SLOT, MORE, COUNTS = range(64, 74)
+STATUS, SOURCE_LAYER, SOURCE_SLOT, WANTED, FULL, DEEP, DEVICE, SLOT, MORE = range(9)
+COUNTS = 16
+GATES = 32
 READY, WAITS = 1.0, 2.0
 
 f32 = jnp.float32
@@ -96,8 +98,8 @@
         copy.wait()
 
 
-def rows_body(table_ref, state_ref, raw_ref):
-    select = selection(ranked([table_ref[...].astype(f32)])[0], raw_ref.shape[0])
+def rows_body(skip, table_ref, state_ref, raw_ref):
+    select = selection(ranked([table_ref[...].astype(f32)])[0] - skip, raw_ref.shape[0])
     raw_ref[...] = jnp.dot(select.astype(bf16), state_ref[...], preferred_element_type=f32).astype(bf16)
 
 
@@ -127,7 +129,7 @@
     return sum(jnp.where((layer ^ r) == other, float(other), 0.0) for other in range(sections))
 
 
-def meta_body(few, index_ref, *refs):
+def meta_body(few, skip, index_ref, *refs):
     tables, (gates_ref, raw_ref, payload_ref) = refs[:-3], refs[-3:]
     layer, member = index_ref[0], index_ref[1]
     count, width = raw_ref.shape
@@ -154,23 +156,24 @@
     gates = gates_ref[...]
     high = gates.astype(bf16).astype(f32)
     named = {STATUS: status, SOURCE_LAYER: source_layer, SOURCE_SLOT: source_slot, WANTED: wanted}
-    summed = {FULL: full, DEEP: deep}
-    summed.update({COUNTS + place: row for place, row in enumerate(counts)})
+    named.update({FULL: full, DEEP: deep})
+    named.update({COUNTS + place: row for place, row in enumerate(counts)})
     for expert in range(gates.shape[0]):
-        named[expert] = high[expert:expert + 1]
-        named[gates.shape[0] + expert] = (gates - high)[expert:expert + 1]
-    select = selection(ranks[0], count)
-    across_tokens = (((1,), (1,)), ((), ()))
-
-    def lanes(left, rows):
-        empty = jnp.zeros_like(deep)
-        table = stack_rows([rows.get(lane, empty) for lane in range(LANES)]).astype(bf16)
-        return lax.dot_general(left.astype(bf16), table, across_tokens, preferred_element_type=f32)
-
+        named[GATES + expert] = high[expert:expert + 1]
+        named[GATES + gates.shape[0] + expert] = (gates - high)[expert:expert + 1]
+    last = -(-(max(named) + 1) // 8) * 8
+    empty = jnp.zeros_like(deep)
+    table = [named.get(number, empty) for number in range(last)]
+    table = stack_rows(table + [jnp.zeros((LANES - last, deep.shape[1]), f32)]).astype(bf16)
+    select = selection(ranks[0] - skip, count)
+    left = stack_rows([select, jnp.ones_like(select)]).astype(bf16)
+    both = lax.dot_general(left, table, (((1,), (1,)), ((), ())), preferred_element_type=f32)
     lane = iota((count, LANES), 1)
-    extra = lanes(select, named) + lanes(jnp.ones_like(select), summed)
+    by_column = jnp.logical_or(lane == FULL, lane == DEEP)
+    by_column = jnp.logical_or(by_column, jnp.logical_and(lane >= COUNTS, lane < GATES))
+    extra = jnp.where(by_column, both[count:], both[:count])
     extra = jnp.where(lane == DEVICE, jnp.full((count, LANES), member + 1, jnp.int32).astype(f32), extra)
-    extra = jnp.where(lane == SLOT, (iota((count, LANES), 0) + 1).astype(f32), extra)
+    extra = jnp.where(lane == SLOT, (iota((count, LANES), 0) + (1 + skip)).astype(f32), extra)
     payload_ref[:, :width] = raw_ref[...]
     payload_ref[:, width:] = extra.astype(bf16)
 
@@ -188,6 +191,28 @@
             rows_ref[place * count:(place + 1) * count] = block
     else:
         rows_ref[...] = stack_rows([block.astype(f32) for block in blocks]).astype(bf16)
+
+
+def pair_body(*refs):
+    out_ref = refs[-1]
+    for q in range(out_ref.shape[0]):
+        out_ref[q] = refs[q][...]
+
+
+def more_stack_body(half, rows_ref, *refs):
+    near, pair_ref, into_ref = refs[:half], refs[half], refs[half + 1]
+    more = [ref[...] for ref in near] + [pair_ref[q] for q in range(half)]
+    count = more[0].shape[0]
+    if count % 16 == 0:
+        for place, block in enumerate(more):
+            into_ref[2 * place * count:(2 * place + 1) * count] = rows_ref[place * count:(place + 1) * count]
+            into_ref[(2 * place + 1) * count:(2 * place + 2) * count] = block
+        return
+    rows = rows_ref[...].astype(f32)
+    stacked = []
+    for place, block in enumerate(more):
+        stacked += [rows[place * count:(place + 1) * count], block.astype(f32)]
+    into_ref[...] = stack_rows(stacked).astype(bf16)
 
 
 def first_pass_body(half, sections, count, flight, member_ref, *refs):
@@ -200,9 +225,10 @@
     total = jnp.sum(jnp.where(lane_of(extra, SLOT) == 1.0, extra, 0.0), axis=0, keepdims=True)
     total = jnp.max(total[:, COUNTS:COUNTS + sections], axis=1, keepdims=True)
     wanted_count = part_ref.shape[0]
-    mode = sum(jnp.where(total > limit, 1, 0) for limit in (wanted_count // 4, wanted_count // 2, wanted_count))
-    mode = jnp.where(lane_of(most, DEEP) > 0.5, 3, mode)
-    mode_ref[...] = jnp.where(lane_of(most, FULL) > 0.5, 4, mode)
+    mode = jnp.where(total > wanted_count // 4, 1, 0) + jnp.where(total > wanted_count // 2, 1, 0)
+    again = jnp.where(total > wanted_count // 2, 4, 3)
+    again = jnp.where(total > wanted_count, again, jnp.where(lane_of(most, DEEP) > 0.5, again, mode))
+    mode_ref[...] = jnp.where(lane_of(most, FULL) > 0.5, 5, again)
 
 
 def activated(rows, gate_ref, up_ref):
@@ -214,7 +240,7 @@
 def weight_of(extra, member, flight):
     lane = iota(extra.shape, 1)
     expert = member // GROUP
-    mine = jnp.logical_or(lane == expert, lane == flight + expert)
+    mine = jnp.logical_or(lane == GATES + expert, lane == GATES + flight + expert)
     return jnp.sum(jnp.where(mine, extra, 0.0), axis=1, keepdims=True)
 
 
@@ -475,14 +501,49 @@
     mib = 2**20
     chunks = next(c for c in (7, 8, 4, 2, 1) if width % (c * LANES) == 0)
 
-    def payload_of(count, raw, gate_weights):
+    def raw_of(count, skip):
         return call(
-            functools.partial(meta_body, few),
+            functools.partial(rows_body, skip),
+            shape((count, width), bf16),
+            2,
+            traffic=2 * tokens * width,
+            limit=8 * mib,
+        )(table, state)
+
+    def payload_of(raw, gate_weights, skip):
+        count = raw.shape[0]
+        return call(
+            functools.partial(meta_body, few, skip),
             shape((count, width + LANES), bf16),
             sections + 2,
             scalars=1,
             limit=8 * mib,
         )(index, *tables, gate_weights, raw)
+
+    def near_of(payload):
+        return [payload] + [passed(payload, "expert", r) for r in range(2, devices, 2)]
+
+    def pair_of(near, after=()):
+        count = near[0].shape[0]
+        stacked = call(
+            pair_body,
+            shape((half, *near[0].shape), bf16),
+            half + len(after),
+            traffic=4 * half * count * width,
+            limit=4 * mib + 8 * half * count * width,
+        )(*near, *after)
+        return passed(stacked, "expert", 1)
+
+    def held(after, *weights):
+        return call(
+            held_body,
+            tuple(shape(w.shape, bf16) for w in weights),
+            1,
+            streamed=len(weights),
+            scratch=[pltpu.SemaphoreType.DMA((len(weights),))],
+            traffic=4 * sum(w.size for w in weights),
+            limit=2 * sum(w.size for w in weights) + 2 * mib,
+        )(after, *weights)
 
     def pass_shapes(size, wanted):
         return (
@@ -520,9 +581,9 @@
             limit=apply_limit(size, wanted),
         )(layer, rows, sent, *changed)
 
-    def passes(rows, count, weights):
-        size = devices * count
-        wanted = 2 * count
+    def passes(rows, wanted, weights):
+        size = rows.shape[0]
+        count = size // devices
         part, chosen, sent = call(
             functools.partial(pass_body, count, flight),
             pass_shapes(size, wanted),
@@ -607,34 +668,25 @@
         )(layer, *blocks, *tables, state)
         return new_state, gram
 
-    def looped(rows, more, count, weights):
+    def looped(rows, more, weights):
         _, rows = lax.while_loop(
             lambda carry: carry[0][0, 0] > 0.5,
-            lambda carry: passes(carry[1], count, weights)[::-1],
+            lambda carry: passes(carry[1], few, weights)[::-1],
             (more, rows),
         )
-        return finish(rows, count, weights)
+        return finish(rows, rows.shape[0] // devices, weights)
 
     table, kept_routes = call(
         functools.partial(table_body, flight), (shape((1, tokens), bf16), shape(routes.shape, routes.dtype)), 1
     )(routes)
     tables = exchanged(table, "layer")
-    raw = call(
-        rows_body, shape((few, width), bf16), 2, traffic=2 * tokens * width, limit=8 * mib
-    )(table, state)
+    raw = raw_of(few, 0)
     gate_weights = call(gates_body, shape((flight, tokens), f32), 2)(kept_routes, gates)
-    payload = payload_of(few, raw, gate_weights)
-    near = [payload] + [passed(payload, "expert", r) for r in range(2, devices, 2)]
-    pair = passed(jnp.stack(near), "expert", 1)
-    weights = call(
-        held_body,
-        tuple(shape(w.shape, bf16) for w in (w_gate, w_up, w_down)),
-        1,
-        streamed=3,
-        scratch=[pltpu.SemaphoreType.DMA((3,))],
-        traffic=12 * w_gate.size,
-        limit=6 * w_gate.size + 2 * mib,
-    )(near[1], w_gate, w_up, w_down)
+    payload = payload_of(raw, gate_weights, 0)
+    near = near_of(payload)
+    early = held(payload, w_gate)
+    pair = pair_of(near, early)
+    weights = *early, *held(near[1], w_up, w_down)
     size = devices * few
     rows, mode, part, chosen, sent = call(
         functools.partial(first_pass_body, half, sections, few, flight),
@@ -653,28 +705,29 @@
 
         return run
 
-    def again(rows, part, chosen, sent, gate_weights, *weights):
-        rows, more = applied(rows, sent, summed(part, chosen))
-        return looped(rows, more, few, weights)
+    def again(share):
+        def run(rows, part, chosen, sent, gate_weights, *weights):
+            wanted = part.shape[0] // share
+            rows, more = applied(rows, sent, summed(part[:wanted], chosen[:wanted]))
+            return looped(rows, more, weights)
+
+        return run
 
     def filled(rows, part, chosen, sent, gate_weights, *weights):
         most = fronts * CAP * flight
-        raw = call(
-            rows_body, shape((most, width), bf16), 2, traffic=2 * tokens * width, limit=8 * mib
-        )(table, state)
-        payload = payload_of(most, raw, gate_weights)
-        near = [payload] + [passed(payload, "expert", r) for r in range(2, devices, 2)]
+        near = near_of(payload_of(raw_of(most - few, few), gate_weights, few))
         rows = call(
-            functools.partial(stack_body, half),
+            functools.partial(more_stack_body, half),
             shape((devices * most, width + LANES), bf16),
-            half + 1,
+            half + 2,
             traffic=4 * devices * most * width,
             limit=4 * mib + 16 * devices * most * width,
-        )(*near, passed(jnp.stack(near), "expert", 1))
-        return looped(rows, jnp.ones((1, 1), f32), most, weights)
+        )(rows, *near, pair_of(near))
+        rows, more = passes(rows, 4 * few, weights)
+        return looped(rows, more, weights)
 
     state, gram = lax.switch(
-        mode[0, 0], (once(4), once(2), once(1), again, filled), rows, part, chosen, sent, gate_weights, *weights
+        mode[0, 0], (once(4), once(2), once(1), again(2), again(1), filled), rows, part, chosen, sent, gate_weights, *weights
     )
     return state.reshape(1, fronts, tok_rows, width), gram[None]
 

time: 64.3 us -> 62.4 us (0.970); the launches traced: 63.1 us -> 62.2 us
  local copies, waits for them, and re-layouts: 6.25 us -> 2.98 us
  starting transfers between devices: 23.9 us -> 26.7 us
    unnamed x14, local copies, waits for them, and re-layouts: 6.23 us -> 2.96 us
    ppermute x20, starting transfers between devices: 23.9 us -> 26.7 us  [passed(): lax.ppermute(value, axis, [(i, i ^ r) for i in range(lax.axis_size(axis))])]
    pallas_call x3 -> x5, Pallas kernels: 2.71 us -> 2.73 us  [the longest x1 1.51 us: raw_of(): call(functools.partial(rows_body, skip), shape((count, width), bf16), 2,...]
where the time goes in v2:
time: 62.4 us; the launch traced here: 62.2 us
  starting transfers between devices  26.7 us (43%)
  waiting for transfers between devices  21 us (34%)
  Pallas kernels  9.52 us (15%)
  local copies, waits for them, and re-layouts  2.98 us (5%)
  between operations  1.54 us (2%)
    ppermute x20, starting transfers between devices, passed(): lax.ppermute(value, axis, [(i, i ^ r) for i in range(lax.axis_size(axis))])  26.7 us
    ppermute x20, waiting for transfers between devices, passed(): lax.ppermute(value, axis, [(i, i ^ r) for i in range(lax.axis_size(axis))])  21 us
    unnamed x14, local copies, waits for them, and re-layouts  2.96 us
    pallas_call x1, Pallas kernels, finish(): call(functools.partial(gram_body, scale, width), shape((units, GROUP * un...  1.81 us
    pallas_call x1, Pallas kernels, shards(): call(functools.partial(first_pass_body, half, sections, few, flight), (sh...  1.71 us
    pallas_call x1, Pallas kernels, finish(): call(body, (shape((size, units), bf16), shape((count, width), bf16), shap...  1.55 us
    pallas_call x1, Pallas kernels, raw_of(): call(functools.partial(rows_body, skip), shape((count, width), bf16), 2,...  1.51 us
    pallas_call x1, Pallas kernels, finish(): call(functools.partial(merge_body, sections), shape((tokens, width), bf16...  1.43 us
  transfers between devices with their start and end apart: 20, of which 11 were waited for; matrix products, arithmetic and copies ran while one was open for 0% of the time, Pallas kernels for 6%

profile of v2, /device:TPU:1, one launch (start us, length us, event | category | flops | bytes accessed | tf_op | source)
XLA Modules:
  0.0 62.2 jit_solution(4552521209598553872)
XLA Ops:
  0.6 0.7 %copy-done.3 = s32[1,4,32,8]{2,3,1,0:T(8,128)S(1)} copy-done((s32[1,4,32,8]{2,3,1,0:T(8,128)S(1)}, s32[1,4,32,8]{2,3,1,0:T(8,128)}, u32[]{:S(2)}) %copy-start.3) | copy-done | bytes 4120
  1.3 0.1 shard_map.98
  1.4 2.6 %collective-permute-start.102 = (bf16[1,128]{1,0:T(2,128)(2,1)S(1)}, bf16[1,128]{1,0:T(2,128)(2,1)S(1)}, u32[]{:S(2)}, u32[]{:S(2)}) collective-permute-start(bf16[1,128]{1,0:T(2,128)(2,1)S(1)} %get-tuple-element.475.table_ref.refs_0_), channel_id=1, source_target_pairs={{0,24},{8,16},{16,8},{24,0},{1,25},{9,17},{17,9},{25,1},{2,26},{10... | collective-permute-start | bytes 776 | tf_op jit(solution)/shard_map/ppermute | solution.py:476
  4.1 0.5 collective-permute-start.100
  4.5 0.1 pad_add_fusion.index_ref
  4.6 1.5 %shard_map.100.refs_5_ = bf16[4,3584]{1,0:T(4,128)(2,1)S(1)} custom-call(bf16[1,128]{1,0:T(2,128)(2,1)S(1)} %get-tuple-element.475.table_ref.refs_0_, bf16[128,3584]{1,0:T(8,128)(2,1)} %bitcast.33), custom_call_target="tpu_custom_call" | custom-call | bytes 917504 | tf_op jit(solution)/shard_map/pallas_call | solution.py:505
  6.1 0.0 copy-start.4
  6.1 0.7 %copy-done.4 = f32[1,4,32,8]{2,3,1,0:T(8,128)S(1)} copy-done((f32[1,4,32,8]{2,3,1,0:T(8,128)S(1)}, f32[1,4,32,8]{2,3,1,0:T(8,128)}, u32[]{:S(2)}) %copy-start.4) | copy-done | bytes 4120
  6.9 0.1 shard_map.99.refs_4_
  6.9 0.0 collective-permute-done.102.refs_3_
  6.9 0.0 collective-permute-done.101.refs_2_
  7.0 0.8 %shard_map.101.after_ref.refs_0_ = bf16[4,3712]{1,0:T(4,128)(2,1)S(1)} custom-call(s32[2]{0:T(128)S(1)} %pad_add_fusion.index_ref, bf16[1,128]{1,0:T(2,128)(2,1)S(1)} %get-tuple-element.475.table_ref.refs_0_, bf16[1,128]{1,0:T(2,128)(2,1)S(1)} %collective-permute-done.100.refs_1_, bf16[1,128]{1,0:T(2,128)(2,1)S(1)} %collective-permute-done.101.refs_2_, ...), custom_call_target="tpu_custom_call" | custom-call | tf_op jit(solution)/shard_map/pallas_call | solution.py:515
  7.8 3.3 %collective-permute-start.105 = (bf16[4,3712]{1,0:T(4,128)(2,1)S(1)}, bf16[4,3712]{1,0:T(4,128)(2,1)S(1)}, u32[]{:S(2)}, u32[]{:S(2)}) collective-permute-start(bf16[4,3712]{1,0:T(4,128)(2,1)S(1)} %shard_map.101.after_ref.refs_0_), channel_id=1, source_target_pairs={{0,6},{1,7},{2,4},{3,5},{4,2},{5,3},{6,0},{7,1},{8,14},{9,15},{10,... | collective-permute-start | bytes 89096 | tf_op jit(solution)/shard_map/ppermute | solution.py:476
  11.1 0.3 collective-permute-start.103
  11.4 1.5 %copy-done = bf16[1,3584,256]{2,1,0:T(8,128)(2,1)S(1)} copy-done((bf16[1,3584,256]{2,1,0:T(8,128)(2,1)S(1)}, bf16[1,3584,256]{2,1,0:T(8,128)(2,1)}, u32[]{:S(2)}) %copy-start) | copy-done | bytes 1835032
  12.9 0.1 shard_map.102.refs_4_.refs_6_
  13.1 2.0 %collective-permute-done.104.refs_2_ = bf16[4,3712]{1,0:T(4,128)(2,1)S(1)} collective-permute-done((bf16[4,3712]{1,0:T(4,128)(2,1)S(1)}, bf16[4,3712]{1,0:T(4,128)(2,1)S(1)}, u32[]{:S(2)}, u32[]{:S(2)}) %collective-permute-start.104) | collective-permute-done | bytes 29728 | tf_op jit(solution)/shard_map/ppermute | solution.py:476
  15.1 0.0 copy-start.6
  15.1 1.3 %collective-permute-start.106 = (bf16[4,4,3712]{2,1,0:T(4,128)(2,1)S(1)}, bf16[4,4,3712]{2,1,0:T(4,128)(2,1)S(1)}, u32[]{:S(2)}, u32[]{:S(2)}) collective-permute-start(bf16[4,4,3712]{2,1,0:T(4,128)(2,1)S(1)} %shard_map.103), channel_id=1, source_target_pairs={{0,1},{1,0},{2,3},{3,2},{4,5},{5,4},{6,7},{7,6},{8,9},{9,8},{10,11... | collective-permute-start | bytes 356360 | tf_op jit(solution)/shard_map/ppermute | solution.py:476
  16.4 0.3 shard_map.104
  16.6 2.2 %collective-permute-done.106.refs_4_ = bf16[4,4,3712]{2,1,0:T(4,128)(2,1)S(1)} collective-permute-done((bf16[4,4,3712]{2,1,0:T(4,128)(2,1)S(1)}, bf16[4,4,3712]{2,1,0:T(4,128)(2,1)S(1)}, u32[]{:S(2)}, u32[]{:S(2)}) %collective-permute-start.106) | collective-permute-done | bytes 118816 | tf_op jit(solution)/shard_map/ppermute | solution.py:476
  18.8 1.7 %shard_map.105 = (bf16[32,3712]{1,0:T(8,128)(2,1)S(1)}, s32[1,1]{1,0:T(1,128)}, bf16[8,3584]{1,0:T(8,128)(2,1)S(1)}, bf16[8,3712]{1,0:T(8,128)(2,1)S(1)}, f32[1,32]{1,0:T(1,128)S(1)}) custom-call(s32[1]{0:T(128)} %bitcast.15.member_ref, bf16[4,3712]{1,0:T(4,128)(2,1)S(1)} %shard_map.101.after_ref.refs_0_, ...), custom_call_target="tpu_custom_call" | custom-call | flops 44040192 | bytes 458752 | tf_op jit(solution)/shard_map/pallas_call | solution.py:691
  21.2 40.8 %conditional.1 = (bf16[1,4,32,3584]{3,2,1,0:T(8,128)(2,1)}, f32[1,256,2048]{2,1,0:T(8,128)}) conditional(s32[]{:T(128)} %bitcast.25, (bf16[8,3584]{1,0:T(8,128)(2,1)S(1)}, bf16[8,3712]{1,0:T(8,128)(2,1)S(1)}, s32[1]{0:T(128)}, s32[1]{0:T(128)}, bf16[32,3712]{1,0:T(8,128)(2,1)S(1)}, /*index=5*/f32[1,32]{1,0:T(1,128)S(1)}, ...), branch_computations={%region_0.0_spmd, %region_1.0_spmd, %region_2.0_spmd, %region_3.0_... | conditional | flops 566231040 | bytes 25121840 | solution.py:729
  21.3 1.3 %collective-permute-start.13 = (bf16[4,3584]{1,0:T(4,128)(2,1)S(1)}, bf16[4,3584]{1,0:T(4,128)(2,1)S(1)}, u32[]{:S(2)}, u32[]{:S(2)}) collective-permute-start(bf16[4,3584]{1,0:T(4,128)(2,1)S(1)} %slice.14.a_ref), channel_id=1, source_target_pairs={{0,1},{1,0},{2,3},{3,2},{4,5},{5,4},{6,7},{7,6},{8,9},{9,8},{10,11... | collective-permute-start | bytes 86024 | tf_op jit(solution)/shard_map/cond/branch_1_fun/ppermute | solution.py:476
  22.5 1.5 %collective-permute-done.13.b_ref = bf16[4,3584]{1,0:T(4,128)(2,1)S(1)} collective-permute-done((bf16[4,3584]{1,0:T(4,128)(2,1)S(1)}, bf16[4,3584]{1,0:T(4,128)(2,1)S(1)}, u32[]{:S(2)}, u32[]{:S(2)}) %collective-permute-start.13) | collective-permute-done | bytes 28704 | tf_op jit(solution)/shard_map/cond/branch_1_fun/ppermute | solution.py:476
  24.1 0.1 collective-permute-start.14
  24.1 2.7 %collective-permute-done.14.b_ref = bf16[4,3584]{1,0:T(4,128)(2,1)S(1)} collective-permute-done((bf16[4,3584]{1,0:T(4,128)(2,1)S(1)}, bf16[4,3584]{1,0:T(4,128)(2,1)S(1)}, u32[]{:S(2)}, u32[]{:S(2)}) %collective-permute-start.14) | collective-permute-done | bytes 28704 | tf_op jit(solution)/shard_map/cond/branch_1_fun/ppermute | solution.py:476
  26.9 1.3 %collective-permute-start.15 = (bf16[4,3584]{1,0:T(4,128)(2,1)S(1)}, bf16[4,3584]{1,0:T(4,128)(2,1)S(1)}, u32[]{:S(2)}, u32[]{:S(2)}) collective-permute-start(bf16[4,3584]{1,0:T(4,128)(2,1)S(1)} %branch_1_fun.9.a_ref), channel_id=1, source_target_pairs={{0,4},{1,5},{2,6},{3,7},{4,0},{5,1},{6,2},{7,3},{8,12},{9,13},{10,... | collective-permute-start | bytes 86024 | tf_op jit(solution)/shard_map/cond/branch_1_fun/ppermute | solution.py:476
  28.2 2.7 %collective-permute-done.15.b_ref = bf16[4,3584]{1,0:T(4,128)(2,1)S(1)} collective-permute-done((bf16[4,3584]{1,0:T(4,128)(2,1)S(1)}, bf16[4,3584]{1,0:T(4,128)(2,1)S(1)}, u32[]{:S(2)}, u32[]{:S(2)}) %collective-permute-start.15) | collective-permute-done | bytes 28704 | tf_op jit(solution)/shard_map/cond/branch_1_fun/ppermute | solution.py:476
  30.9 6.9 %collective-permute-start.18 = (bf16[4,3712]{1,0:T(4,128)(2,1)S(1)}, bf16[4,3712]{1,0:T(4,128)(2,1)S(1)}, u32[]{:S(2)}, u32[]{:S(2)}) collective-permute-start(bf16[4,3712]{1,0:T(4,128)(2,1)S(1)} %branch_1_fun.10.refs_0_), channel_id=1, source_target_pairs={{0,24},{8,16},{16,8},{24,0},{1,25},{9,17},{17,9},{25,1},{2,26},{10... | collective-permute-start | bytes 89096 | tf_op jit(solution)/shard_map/cond/branch_1_fun/ppermute | solution.py:476
  37.8 0.4 collective-permute-start.17
  38.2 0.1 collective-permute-start.16
  38.3 1.6 %collective-permute-done.18.refs_3_ = bf16[4,3712]{1,0:T(4,128)(2,1)S(1)} collective-permute-done((bf16[4,3712]{1,0:T(4,128)(2,1)S(1)}, bf16[4,3712]{1,0:T(4,128)(2,1)S(1)}, u32[]{:S(2)}, u32[]{:S(2)}) %collective-permute-start.18) | collective-permute-done | bytes 29728 | tf_op jit(solution)/shard_map/cond/branch_1_fun/ppermute | solution.py:476
  39.9 0.7 %collective-permute-done.17.refs_2_ = bf16[4,3712]{1,0:T(4,128)(2,1)S(1)} collective-permute-done((bf16[4,3712]{1,0:T(4,128)(2,1)S(1)}, bf16[4,3712]{1,0:T(4,128)(2,1)S(1)}, u32[]{:S(2)}, u32[]{:S(2)}) %collective-permute-start.17) | collective-permute-done | bytes 29728 | tf_op jit(solution)/shard_map/cond/branch_1_fun/ppermute | solution.py:476
  40.5 1.5 %branch_1_fun.11 = (bf16[32,256]{1,0:T(8,128)(2,1)S(1)}, bf16[4,3584]{1,0:T(4,128)(2,1)S(1)}, bf16[16,3584]{1,0:T(8,128)(2,1)S(1)}, bf16[16,4096]{1,0:T(8,128)(2,1)S(1)}) custom-call(s32[1]{0:T(128)} %get-tuple-element.299.layer_ref, s32[1]{0:T(128)} %get-tuple-element.300.member_ref, bf16[32,3712]{1,0:T(8,128)(2,1)S(1)} %get-tuple-element.301.rows_ref, ...), custom_call_target="tpu_custom_call" | custom-call | flops 176160768 | bytes 5505024 | tf_op jit(solution)/shard_map/cond/branch_1_fun/pallas_call | solution.py:608
  42.1 1.3 %collective-permute-start.19 = (bf16[16,4096]{1,0:T(8,128)(2,1)S(1)}, bf16[16,4096]{1,0:T(8,128)(2,1)S(1)}, u32[]{:S(2)}, u32[]{:S(2)}) collective-permute-start(bf16[16,4096]{1,0:T(8,128)(2,1)S(1)} %get-tuple-element.310), channel_id=1, source_target_pairs={{0,1},{1,0},{2,3},{3,2},{4,5},{5,4},{6,7},{7,6},{8,9},{9,8},{10,11... | collective-permute-start | bytes 393224 | tf_op jit(solution)/shard_map/cond/branch_1_fun/ppermute | solution.py:476
  43.4 3.6 %collective-permute-done.19.far_ref = bf16[16,4096]{1,0:T(8,128)(2,1)S(1)} collective-permute-done((bf16[16,4096]{1,0:T(8,128)(2,1)S(1)}, bf16[16,4096]{1,0:T(8,128)(2,1)S(1)}, u32[]{:S(2)}, u32[]{:S(2)}) %collective-permute-start.19) | collective-permute-done | bytes 131104 | tf_op jit(solution)/shard_map/cond/branch_1_fun/ppermute | solution.py:476
  47.0 0.1 branch_1_fun.12
  47.0 0.1 collective-permute-start.20
  47.1 1.7 %collective-permute-start.21 = (bf16[4,7680]{1,0:T(4,128)(2,1)S(1)}, bf16[4,7680]{1,0:T(4,128)(2,1)S(1)}, u32[]{:S(2)}, u32[]{:S(2)}) collective-permute-start(bf16[4,7680]{1,0:T(4,128)(2,1)S(1)} %get-tuple-element.314), channel_id=1, source_target_pairs={{0,4},{1,5},{2,6},{3,7},{4,0},{5,1},{6,2},{7,3},{8,12},{9,13},{10,... | collective-permute-start | bytes 184328 | tf_op jit(solution)/shard_map/cond/branch_1_fun/ppermute | solution.py:476
  48.8 1.8 %collective-permute-start.22 = (bf16[4,7680]{1,0:T(4,128)(2,1)S(1)}, bf16[4,7680]{1,0:T(4,128)(2,1)S(1)}, u32[]{:S(2)}, u32[]{:S(2)}) collective-permute-start(bf16[4,7680]{1,0:T(4,128)(2,1)S(1)} %get-tuple-element.315), channel_id=1, source_target_pairs={{0,6},{1,7},{2,4},{3,5},{4,2},{5,3},{6,0},{7,1},{8,14},{9,15},{10,... | collective-permute-start | bytes 184328 | tf_op jit(solution)/shard_map/cond/branch_1_fun/ppermute | solution.py:476
  50.6 0.5 collective-permute-done.21.refs_2_.refs_1_
  51.1 3.0 %collective-permute-done.22.refs_3_.refs_2_ = bf16[4,7680]{1,0:T(4,128)(2,1)S(1)} collective-permute-done((bf16[4,7680]{1,0:T(4,128)(2,1)S(1)}, bf16[4,7680]{1,0:T(4,128)(2,1)S(1)}, u32[]{:S(2)}, u32[]{:S(2)}) %collective-permute-start.22) | collective-permute-done | bytes 61472 | tf_op jit(solution)/shard_map/cond/branch_1_fun/ppermute | solution.py:476
  54.2 3.0 %collective-permute-start.25 = (bf16[4,3584]{1,0:T(4,128)(2,1)S(1)}, bf16[4,3584]{1,0:T(4,128)(2,1)S(1)}, u32[]{:S(2)}, u32[]{:S(2)}) collective-permute-start(bf16[4,3584]{1,0:T(4,128)(2,1)S(1)} %branch_1_fun.13.refs_0_), channel_id=1, source_target_pairs={{0,24},{8,16},{16,8},{24,0},{1,25},{9,17},{17,9},{25,1},{2,26},{10... | collective-permute-start | bytes 86024 | tf_op jit(solution)/shard_map/cond/branch_1_fun/ppermute | solution.py:476
  57.2 0.7 %collective-permute-start.24 = (bf16[4,3584]{1,0:T(4,128)(2,1)S(1)}, bf16[4,3584]{1,0:T(4,128)(2,1)S(1)}, u32[]{:S(2)}, u32[]{:S(2)}) collective-permute-start(bf16[4,3584]{1,0:T(4,128)(2,1)S(1)} %branch_1_fun.13.refs_0_), channel_id=1, source_target_pairs={{0,16},{8,24},{16,0},{24,8},{1,17},{9,25},{17,1},{25,9},{2,18},{10... | collective-permute-start | bytes 86024 | tf_op jit(solution)/shard_map/cond/branch_1_fun/ppermute | solution.py:476
  57.9 1.8 %branch_1_fun.15 = f32[256,2048]{1,0:T(8,128)} custom-call(s32[1]{0:T(128)} %get-tuple-element.300.member_ref, bf16[32,256]{1,0:T(8,128)(2,1)S(1)} %get-tuple-element.311.hidden_ref.mine_ref, bf16[16,4096]{1,0:T(8,128)(2,1)S(1)} %collective-permute-done.19.far_ref, bf16[4,7680]{1,0:T(4,128)(2,1)S(1)} %collective-permute-done.20.refs_1_.refs_0_, ...), custom_call_target="tpu_custom_call" | custom-call | flops 33554432 | bytes 2097152 | tf_op jit(solution)/shard_map/cond/branch_1_fun/pallas_call | solution.py:648
  59.7 0.6 collective-permute-done.24.refs_2_
  60.3 1.4 %branch_1_fun.14 = bf16[128,3584]{1,0:T(8,128)(2,1)} custom-call(s32[1]{0:T(128)} %get-tuple-element.299.layer_ref, bf16[4,3584]{1,0:T(4,128)(2,1)S(1)} %branch_1_fun.13.refs_0_, bf16[4,3584]{1,0:T(4,128)(2,1)S(1)} %collective-permute-done.23.refs_1_, bf16[4,3584]{1,0:T(4,128)(2,1)S(1)} %collective-permute-done.24.refs_2_, ...), custom_call_target="tpu_custom_call" | custom-call | bytes 1835008 | tf_op jit(solution)/shard_map/cond/branch_1_fun/pallas_call | solution.py:659
  (26 shorter events, 0.2 us)
Async XLA Ops:
  0.6 0.7 %copy-start.3 = (s32[1,4,32,8]{2,3,1,0:T(8,128)S(1)}, s32[1,4,32,8]{2,3,1,0:T(8,128)}, u32[]{:S(2)}) copy-start(s32[1,4,32,8]{2,3,1,0:T(8,128)} %param.24) | copy-start | bytes 12292
  1.4 5.5 %collective-permute-start.102 = (bf16[1,128]{1,0:T(2,128)(2,1)S(1)}, bf16[1,128]{1,0:T(2,128)(2,1)S(1)}, u32[]{:S(2)}, u32[]{:S(2)}) collective-permute-start(bf16[1,128]{1,0:T(2,128)(2,1)S(1)} %get-tuple-element.475.table_ref.refs_0_), channel_id=1, source_target_pairs={{0,24},{8,16},{16,8},{24,0},{1,25},{9,17},{17,9},{25,1},{2,26},{10... | collective-permute-start | bytes 776 | tf_op jit(solution)/shard_map/ppermute | solution.py:476
  4.1 2.9 %collective-permute-start.101 = (bf16[1,128]{1,0:T(2,128)(2,1)S(1)}, bf16[1,128]{1,0:T(2,128)(2,1)S(1)}, u32[]{:S(2)}, u32[]{:S(2)}) collective-permute-start(bf16[1,128]{1,0:T(2,128)(2,1)S(1)} %get-tuple-element.475.table_ref.refs_0_), channel_id=1, source_target_pairs={{0,16},{8,24},{16,0},{24,8},{1,17},{9,25},{17,1},{25,9},{2,18},{10... | collective-permute-start | bytes 776 | tf_op jit(solution)/shard_map/ppermute | solution.py:476
  4.1 2.9 %collective-permute-start.100 = (bf16[1,128]{1,0:T(2,128)(2,1)S(1)}, bf16[1,128]{1,0:T(2,128)(2,1)S(1)}, u32[]{:S(2)}, u32[]{:S(2)}) collective-permute-start(bf16[1,128]{1,0:T(2,128)(2,1)S(1)} %get-tuple-element.475.table_ref.refs_0_), channel_id=1, source_target_pairs={{0,8},{8,0},{16,24},{24,16},{1,9},{9,1},{17,25},{25,17},{2,10},{10... | collective-permute-start | bytes 776 | tf_op jit(solution)/shard_map/ppermute | solution.py:476
  6.1 0.7 %copy-start.4 = (f32[1,4,32,8]{2,3,1,0:T(8,128)S(1)}, f32[1,4,32,8]{2,3,1,0:T(8,128)}, u32[]{:S(2)}) copy-start(f32[1,4,32,8]{2,3,1,0:T(8,128)} %param.25) | copy-start | bytes 12292
  7.8 5.3 %collective-permute-start.105 = (bf16[4,3712]{1,0:T(4,128)(2,1)S(1)}, bf16[4,3712]{1,0:T(4,128)(2,1)S(1)}, u32[]{:S(2)}, u32[]{:S(2)}) collective-permute-start(bf16[4,3712]{1,0:T(4,128)(2,1)S(1)} %shard_map.101.after_ref.refs_0_), channel_id=1, source_target_pairs={{0,6},{1,7},{2,4},{3,5},{4,2},{5,3},{6,0},{7,1},{8,14},{9,15},{10,... | collective-permute-start | bytes 89096 | tf_op jit(solution)/shard_map/ppermute | solution.py:476
  11.1 4.0 %collective-permute-start.104 = (bf16[4,3712]{1,0:T(4,128)(2,1)S(1)}, bf16[4,3712]{1,0:T(4,128)(2,1)S(1)}, u32[]{:S(2)}, u32[]{:S(2)}) collective-permute-start(bf16[4,3712]{1,0:T(4,128)(2,1)S(1)} %shard_map.101.after_ref.refs_0_), channel_id=1, source_target_pairs={{0,4},{1,5},{2,6},{3,7},{4,0},{5,1},{6,2},{7,3},{8,12},{9,13},{10,... | collective-permute-start | bytes 89096 | tf_op jit(solution)/shard_map/ppermute | solution.py:476
  11.1 4.0 %collective-permute-start.103 = (bf16[4,3712]{1,0:T(4,128)(2,1)S(1)}, bf16[4,3712]{1,0:T(4,128)(2,1)S(1)}, u32[]{:S(2)}, u32[]{:S(2)}) collective-permute-start(bf16[4,3712]{1,0:T(4,128)(2,1)S(1)} %shard_map.101.after_ref.refs_0_), channel_id=1, source_target_pairs={{0,2},{1,3},{2,0},{3,1},{4,6},{5,7},{6,4},{7,5},{8,10},{9,11},{10,... | collective-permute-start | bytes 89096 | tf_op jit(solution)/shard_map/ppermute | solution.py:476
  11.4 1.5 %copy-start = (bf16[1,3584,256]{2,1,0:T(8,128)(2,1)S(1)}, bf16[1,3584,256]{2,1,0:T(8,128)(2,1)}, u32[]{:S(2)}) copy-start(bf16[1,3584,256]{2,1,0:T(8,128)(2,1)} %param.21) | copy-start | bytes 5505028
  12.9 3.4 %copy-start.1 = (bf16[1,3584,256]{2,1,0:T(8,128)(2,1)S(1)}, bf16[1,3584,256]{2,1,0:T(8,128)(2,1)}, u32[]{:S(2)}) copy-start(bf16[1,3584,256]{2,1,0:T(8,128)(2,1)} %param.22) | copy-start | bytes 5505028
  12.9 3.4 %copy-start.2 = (bf16[1,256,3584]{2,1,0:T(8,128)(2,1)S(1)}, bf16[1,256,3584]{2,1,0:T(8,128)(2,1)}, u32[]{:S(2)}) copy-start(bf16[1,256,3584]{2,1,0:T(8,128)(2,1)} %param.23) | copy-start | bytes 5505028
  15.1 3.8 %copy-start.6 = (f32[1,3584]{1,0:T(1,128)S(1)}, f32[1,3584]{1,0:T(1,128)}, u32[]{:S(2)}) copy-start(f32[1,3584]{1,0:T(1,128)} %refs_5_.1) | copy-start | bytes 43012
  15.1 3.8 %collective-permute-start.106 = (bf16[4,4,3712]{2,1,0:T(4,128)(2,1)S(1)}, bf16[4,4,3712]{2,1,0:T(4,128)(2,1)S(1)}, u32[]{:S(2)}, u32[]{:S(2)}) collective-permute-start(bf16[4,4,3712]{2,1,0:T(4,128)(2,1)S(1)} %shard_map.103), channel_id=1, source_target_pairs={{0,1},{1,0},{2,3},{3,2},{4,5},{5,4},{6,7},{7,6},{8,9},{9,8},{10,11... | collective-permute-start | bytes 356360 | tf_op jit(solution)/shard_map/ppermute | solution.py:476
  18.8 2.4 %copy-start.5 = (bf16[4,32,3584]{2,1,0:T(8,128)(2,1)S(1)}, bf16[4,32,3584]{2,1,0:T(8,128)(2,1)}, u32[]{:S(2)}) copy-start(bf16[4,32,3584]{2,1,0:T(8,128)(2,1)} %param.19) | copy-start | bytes 2752516
  21.3 2.8 %collective-permute-start.13 = (bf16[4,3584]{1,0:T(4,128)(2,1)S(1)}, bf16[4,3584]{1,0:T(4,128)(2,1)S(1)}, u32[]{:S(2)}, u32[]{:S(2)}) collective-permute-start(bf16[4,3584]{1,0:T(4,128)(2,1)S(1)} %slice.14.a_ref), channel_id=1, source_target_pairs={{0,1},{1,0},{2,3},{3,2},{4,5},{5,4},{6,7},{7,6},{8,9},{9,8},{10,11... | collective-permute-start | bytes 86024 | tf_op jit(solution)/shard_map/cond/branch_1_fun/ppermute | solution.py:476
  24.1 2.8 %collective-permute-start.14 = (bf16[4,3584]{1,0:T(4,128)(2,1)S(1)}, bf16[4,3584]{1,0:T(4,128)(2,1)S(1)}, u32[]{:S(2)}, u32[]{:S(2)}) collective-permute-start(bf16[4,3584]{1,0:T(4,128)(2,1)S(1)} %branch_1_fun.8.a_ref), channel_id=1, source_target_pairs={{0,2},{1,3},{2,0},{3,1},{4,6},{5,7},{6,4},{7,5},{8,10},{9,11},{10,... | collective-permute-start | bytes 86024 | tf_op jit(solution)/shard_map/cond/branch_1_fun/ppermute | solution.py:476
  26.9 4.0 %collective-permute-start.15 = (bf16[4,3584]{1,0:T(4,128)(2,1)S(1)}, bf16[4,3584]{1,0:T(4,128)(2,1)S(1)}, u32[]{:S(2)}, u32[]{:S(2)}) collective-permute-start(bf16[4,3584]{1,0:T(4,128)(2,1)S(1)} %branch_1_fun.9.a_ref), channel_id=1, source_target_pairs={{0,4},{1,5},{2,6},{3,7},{4,0},{5,1},{6,2},{7,3},{8,12},{9,13},{10,... | collective-permute-start | bytes 86024 | tf_op jit(solution)/shard_map/cond/branch_1_fun/ppermute | solution.py:476
  30.9 9.0 %collective-permute-start.18 = (bf16[4,3712]{1,0:T(4,128)(2,1)S(1)}, bf16[4,3712]{1,0:T(4,128)(2,1)S(1)}, u32[]{:S(2)}, u32[]{:S(2)}) collective-permute-start(bf16[4,3712]{1,0:T(4,128)(2,1)S(1)} %branch_1_fun.10.refs_0_), channel_id=1, source_target_pairs={{0,24},{8,16},{16,8},{24,0},{1,25},{9,17},{17,9},{25,1},{2,26},{10... | collective-permute-start | bytes 89096 | tf_op jit(solution)/shard_map/cond/branch_1_fun/ppermute | solution.py:476
  37.8 2.7 %collective-permute-start.17 = (bf16[4,3712]{1,0:T(4,128)(2,1)S(1)}, bf16[4,3712]{1,0:T(4,128)(2,1)S(1)}, u32[]{:S(2)}, u32[]{:S(2)}) collective-permute-start(bf16[4,3712]{1,0:T(4,128)(2,1)S(1)} %branch_1_fun.10.refs_0_), channel_id=1, source_target_pairs={{0,16},{8,24},{16,0},{24,8},{1,17},{9,25},{17,1},{25,9},{2,18},{10... | collective-permute-start | bytes 89096 | tf_op jit(solution)/shard_map/cond/branch_1_fun/ppermute | solution.py:476
  38.2 2.3 %collective-permute-start.16 = (bf16[4,3712]{1,0:T(4,128)(2,1)S(1)}, bf16[4,3712]{1,0:T(4,128)(2,1)S(1)}, u32[]{:S(2)}, u32[]{:S(2)}) collective-permute-start(bf16[4,3712]{1,0:T(4,128)(2,1)S(1)} %branch_1_fun.10.refs_0_), channel_id=1, source_target_pairs={{0,8},{8,0},{16,24},{24,16},{1,9},{9,1},{17,25},{25,17},{2,10},{10... | collective-permute-start | bytes 89096 | tf_op jit(solution)/shard_map/cond/branch_1_fun/ppermute | solution.py:476
  42.1 4.9 %collective-permute-start.19 = (bf16[16,4096]{1,0:T(8,128)(2,1)S(1)}, bf16[16,4096]{1,0:T(8,128)(2,1)S(1)}, u32[]{:S(2)}, u32[]{:S(2)}) collective-permute-start(bf16[16,4096]{1,0:T(8,128)(2,1)S(1)} %get-tuple-element.310), channel_id=1, source_target_pairs={{0,1},{1,0},{2,3},{3,2},{4,5},{5,4},{6,7},{7,6},{8,9},{9,8},{10,11... | collective-permute-start | bytes 393224 | tf_op jit(solution)/shard_map/cond/branch_1_fun/ppermute | solution.py:476
  47.0 3.6 %collective-permute-start.20 = (bf16[4,7680]{1,0:T(4,128)(2,1)S(1)}, bf16[4,7680]{1,0:T(4,128)(2,1)S(1)}, u32[]{:S(2)}, u32[]{:S(2)}) collective-permute-start(bf16[4,7680]{1,0:T(4,128)(2,1)S(1)} %get-tuple-element.313), channel_id=1, source_target_pairs={{0,2},{1,3},{2,0},{3,1},{4,6},{5,7},{6,4},{7,5},{8,10},{9,11},{10,... | collective-permute-start | bytes 184328 | tf_op jit(solution)/shard_map/cond/branch_1_fun/ppermute | solution.py:476
  47.1 4.0 %collective-permute-start.21 = (bf16[4,7680]{1,0:T(4,128)(2,1)S(1)}, bf16[4,7680]{1,0:T(4,128)(2,1)S(1)}, u32[]{:S(2)}, u32[]{:S(2)}) collective-permute-start(bf16[4,7680]{1,0:T(4,128)(2,1)S(1)} %get-tuple-element.314), channel_id=1, source_target_pairs={{0,4},{1,5},{2,6},{3,7},{4,0},{5,1},{6,2},{7,3},{8,12},{9,13},{10,... | collective-permute-start | bytes 184328 | tf_op jit(solution)/shard_map/cond/branch_1_fun/ppermute | solution.py:476
  48.8 5.3 %collective-permute-start.22 = (bf16[4,7680]{1,0:T(4,128)(2,1)S(1)}, bf16[4,7680]{1,0:T(4,128)(2,1)S(1)}, u32[]{:S(2)}, u32[]{:S(2)}) collective-permute-start(bf16[4,7680]{1,0:T(4,128)(2,1)S(1)} %get-tuple-element.315), channel_id=1, source_target_pairs={{0,6},{1,7},{2,4},{3,5},{4,2},{5,3},{6,0},{7,1},{8,14},{9,15},{10,... | collective-permute-start | bytes 184328 | tf_op jit(solution)/shard_map/cond/branch_1_fun/ppermute | solution.py:476
  54.2 5.5 %collective-permute-start.25 = (bf16[4,3584]{1,0:T(4,128)(2,1)S(1)}, bf16[4,3584]{1,0:T(4,128)(2,1)S(1)}, u32[]{:S(2)}, u32[]{:S(2)}) collective-permute-start(bf16[4,3584]{1,0:T(4,128)(2,1)S(1)} %branch_1_fun.13.refs_0_), channel_id=1, source_target_pairs={{0,24},{8,16},{16,8},{24,0},{1,25},{9,17},{17,9},{25,1},{2,26},{10... | collective-permute-start | bytes 86024 | tf_op jit(solution)/shard_map/cond/branch_1_fun/ppermute | solution.py:476
  57.2 3.1 %collective-permute-start.24 = (bf16[4,3584]{1,0:T(4,128)(2,1)S(1)}, bf16[4,3584]{1,0:T(4,128)(2,1)S(1)}, u32[]{:S(2)}, u32[]{:S(2)}) collective-permute-start(bf16[4,3584]{1,0:T(4,128)(2,1)S(1)} %branch_1_fun.13.refs_0_), channel_id=1, source_target_pairs={{0,16},{8,24},{16,0},{24,8},{1,17},{9,25},{17,1},{25,9},{2,18},{10... | collective-permute-start | bytes 86024 | tf_op jit(solution)/shard_map/cond/branch_1_fun/ppermute | solution.py:476
  57.9 2.4 %collective-permute-start.23 = (bf16[4,3584]{1,0:T(4,128)(2,1)S(1)}, bf16[4,3584]{1,0:T(4,128)(2,1)S(1)}, u32[]{:S(2)}, u32[]{:S(2)}) collective-permute-start(bf16[4,3584]{1,0:T(4,128)(2,1)S(1)} %branch_1_fun.13.refs_0_), channel_id=1, source_target_pairs={{0,8},{8,0},{16,24},{24,16},{1,9},{9,1},{17,25},{25,17},{2,10},{10... | collective-permute-start | bytes 86024 | tf_op jit(solution)/shard_map/cond/branch_1_fun/ppermute | solution.py:476
